TPU v7x, 256 devices: a whole 4x4x8 slice. The times are simulated.
256 devices in a mesh: section: 4 (over x_hi, core), cand: 8 (over z), dp: 8 (over x_lo, y).
Axes of the slice: x: 4 (x_hi: 2, x_lo: 2; x = x_hi * 2 + x_lo), y: 4, z: 8, core: 2. Of those that a mesh axis runs over, the one named last changes fastest.
Arguments:
- inputs: bfloat16 [1024, 8192], P('dp', 'cand'), may hold values from -6 to 6
- parent_gain: float32 [4, 8192], P('section'), may hold values from 0.1 to 1.9
- query_weight: bfloat16 [4, 8192, 4096], P('section', 'dp', 'cand'), may hold values from -0.0625 to 0.0625
- key_value_weight: bfloat16 [4, 2, 8192, 512], P('section', None, 'dp'), may hold values from -0.0625 to 0.0625
- output_weight: bfloat16 [4, 4096, 8192], P('section', 'cand', 'dp'), may hold values from -0.09375 to 0.09375
- candidate_gain: float32 [4, 8, 8192], P('section', 'cand'), may hold values from 0.1 to 1.9
- candidate_down: bfloat16 [4, 8, 64, 8192], P('section', 'cand'), may hold values from -0.0625 to 0.0625
- candidate_up: bfloat16 [4, 8, 64, 8192], P('section', 'cand'), may hold values from -0.75 to 0.75
- kept_ranks: int32 [4, 8], P('section', 'cand'), may hold values from 16 to 64
Outputs:
- states: bfloat16 [4, 1024, 8192], P('section', 'dp', 'cand')
- gradient_down: float32 [4, 8, 64, 8192], P('section', 'cand', None, 'dp')
- gradient_up: float32 [4, 8, 64, 8192], P('section', 'cand', None, 'dp')
Inputs may be any that keep to these rules, and one draw needn't show every extreme that they name: `kept_ranks`: each candidate keeps at least a quarter of its 64 rank components.
All inputs are finite; a program needn't handle non-finite values.
Results may differ from a plain program's by a relative error of at most 0.025.
Values may be sent and summed in bfloat16 or wider, within the bound.
A program may use at most 128 MiB of HBM per device.

v0:
```python
import jax
import jax.numpy as jnp
from jax import lax
from jax.sharding import PartitionSpec as P

D = 8192
HQ = 32
KVH = 4
HD = 128
R = 64
BLK = 64
TOK_DEV = 128


epsilon = 1e-05
rope_base = 500000.0


def shifted(block, axis, distance):
    devices = range(lax.axis_size(axis))
    route = [(i - distance, i) for i in devices if i - distance in devices]
    return lax.ppermute(block, axis, route)


def rotate(matrix, positions):
    half_size = matrix.shape[-1] // 2
    frequency = rope_base ** (-jnp.arange(half_size, dtype=jnp.float32) / half_size)
    angles = positions.astype(jnp.float32)[:, None] * frequency[None, :]
    cosine = jnp.cos(angles)[:, None, :]
    sine_part = jnp.sin(angles)[:, None, :]
    lower_half = matrix[..., :half_size]
    upper_half = matrix[..., half_size:]
    return jnp.concatenate(
        [
            lower_half * cosine - upper_half * sine_part,
            upper_half * cosine + lower_half * sine_part,
        ],
        axis=-1,
    )


def normed(values, gain_row):
    wide = values.astype(jnp.float32)
    inverse_rms = lax.rsqrt(jnp.mean(wide * wide, axis=-1, keepdims=True) + epsilon)
    return (wide * inverse_rms * gain_row).astype(jnp.bfloat16)


def place(buffer, block_rows, offset, active):
    previous = lax.dynamic_slice_in_dim(buffer, offset, block_rows.shape[0], 0)
    chosen = jnp.where(active, block_rows, previous)
    return lax.dynamic_update_slice_in_dim(buffer, chosen, offset, 0)


def candidate_terms(features, produced, gain_row, down_rows, up_rows, rank_mask, token_total):
    cnormed = normed(features, gain_row)
    hidden = (jnp.dot(cnormed, down_rows.T, preferred_element_type=jnp.float32) * rank_mask).astype(
        jnp.bfloat16
    )
    branch = jnp.dot(hidden, up_rows, preferred_element_type=jnp.float32)
    difference = branch - (produced.astype(jnp.float32) - features.astype(jnp.float32))
    scaled = (difference / token_total).astype(jnp.bfloat16)
    gradient_up = jnp.dot(hidden.T, scaled, preferred_element_type=jnp.float32)
    backward = (jnp.dot(scaled, up_rows.T, preferred_element_type=jnp.float32) * rank_mask).astype(
        jnp.bfloat16
    )
    gradient_down = jnp.dot(backward.T, cnormed, preferred_element_type=jnp.float32)
    return (gradient_down, gradient_up)


def shards(
    inputs,
    parent_gain,
    query_weight,
    key_value_weight,
    output_weight,
    candidate_gain,
    candidate_down,
    candidate_up,
    kept_ranks,
):
    candidate_count = lax.axis_size("cand")
    section_count = lax.axis_size("section")
    data_count = lax.axis_size("dp")
    section_index = lax.axis_index("section")
    candidate_index = lax.axis_index("cand")
    head_count = HQ // candidate_count
    groups = HQ // KVH
    value_heads = max(1, head_count // groups)
    shared = head_count // value_heads
    first_head = candidate_index * head_count // groups
    selected = lax.dynamic_slice_in_dim(key_value_weight[0], first_head * HD, value_heads * HD, 2)
    query_full, key_value_full, output_full = (
        lax.all_gather(query_weight[0], "dp", axis=0, tiled=True),
        lax.all_gather(selected, "dp", axis=1, tiled=True),
        lax.all_gather(output_weight[0], "dp", axis=1, tiled=True),
    )
    blocks = TOK_DEV // BLK
    width = inputs.shape[1]
    gain_parent = parent_gain[0]
    gain_candidate = candidate_gain[0, 0]
    down_rows = candidate_down[0, 0]
    up_rows = candidate_up[0, 0]
    rank_mask = (jnp.arange(R) < kept_ranks[0, 0]).astype(jnp.float32)
    token_total = TOK_DEV * data_count
    key_positions = jnp.arange(TOK_DEV)

    def turn(step, carry):
        inbox, key_cache, value_cache, state_rows, input_rows, down_total, up_total = carry
        block_index = step - section_index
        active = (block_index >= 0) & (block_index < blocks)
        offset = jnp.clip(block_index, 0, blocks - 1) * BLK
        first_rows = lax.dynamic_slice_in_dim(inputs, offset, BLK, 0)
        arriving = jnp.where(section_index == 0, first_rows, inbox)
        features = lax.all_gather(arriving, "cand", axis=1, tiled=True)
        normalized = normed(features, gain_parent)
        positions = offset + jnp.arange(BLK)

        def attend(caches):
            queries = jnp.dot(normalized, query_full, preferred_element_type=jnp.float32).reshape(
                BLK, head_count, HD
            )
            queries = (
                rotate(queries, positions)
                .astype(jnp.bfloat16)
                .reshape(BLK, value_heads, shared, HD)
            )
            fresh_keys = jnp.dot(
                normalized, key_value_full[0], preferred_element_type=jnp.float32
            ).reshape(BLK, value_heads, HD)
            fresh_keys = (
                rotate(fresh_keys, positions).astype(jnp.bfloat16).reshape(BLK, value_heads * HD)
            )
            fresh_values = jnp.dot(
                normalized, key_value_full[1], preferred_element_type=jnp.float32
            ).astype(jnp.bfloat16)
            key_rows = lax.dynamic_update_slice_in_dim(caches[0], fresh_keys, offset, 0)
            value_rows = lax.dynamic_update_slice_in_dim(caches[1], fresh_values, offset, 0)
            scores = jnp.einsum(
                "qkgd,skd->kgqs",
                queries,
                key_rows.reshape(TOK_DEV, value_heads, HD),
                preferred_element_type=jnp.float32,
            ) * HD ** (-0.5)
            allowed = key_positions[None, :] <= positions[:, None]
            weights_exp = jnp.where(allowed, jnp.exp(scores), 0.0)
            weights = (weights_exp / jnp.sum(weights_exp, axis=-1, keepdims=True)).astype(
                jnp.bfloat16
            )
            mixed = jnp.einsum(
                "kgqs,skd->qkgd",
                weights,
                value_rows.reshape(TOK_DEV, value_heads, HD),
                preferred_element_type=jnp.float32,
            )
            return (mixed.astype(jnp.bfloat16).reshape(BLK, head_count * HD), key_rows, value_rows)

        def pause(caches):
            return (jnp.zeros((BLK, head_count * HD), jnp.bfloat16), caches[0], caches[1])

        attended, key_cache, value_cache = lax.cond(active, attend, pause, (key_cache, value_cache))
        projected = (
            jnp.dot(attended, output_full, preferred_element_type=jnp.float32)
            .astype(jnp.bfloat16)
            .astype(jnp.float32)
        )
        summed = lax.psum_scatter(
            projected.astype(jnp.bfloat16), "cand", scatter_dimension=1, tiled=True
        ).astype(jnp.float32)
        produced = (arriving.astype(jnp.float32) + summed).astype(jnp.bfloat16)
        state_rows = place(state_rows, produced, offset, active)
        input_rows = place(input_rows, features, offset, active)
        inbox = shifted(produced, "section", 1)
        return (inbox, key_cache, value_cache, state_rows, input_rows, down_total, up_total)

    initial = (
        jnp.zeros((BLK, width), jnp.bfloat16),
        jnp.zeros((TOK_DEV, value_heads * HD), jnp.bfloat16),
        jnp.zeros((TOK_DEV, value_heads * HD), jnp.bfloat16),
        jnp.zeros((TOK_DEV, width), jnp.bfloat16),
        jnp.zeros((TOK_DEV, D), jnp.bfloat16),
        jnp.zeros((R, D), jnp.float32),
        jnp.zeros((R, D), jnp.float32),
    )
    final = lax.fori_loop(0, blocks + section_count - 1, turn, initial)
    state_rows = final[3]
    input_rows = final[4]
    targets = lax.all_gather(state_rows, "cand", axis=1, tiled=True)
    down_total, up_total = candidate_terms(
        input_rows, targets, gain_candidate, down_rows, up_rows, rank_mask, token_total
    )
    down_share, up_share = (
        lax.psum_scatter(
            down_total.astype(jnp.bfloat16), "dp", scatter_dimension=1, tiled=True
        ).astype(jnp.float32),
        lax.psum_scatter(
            up_total.astype(jnp.bfloat16), "dp", scatter_dimension=1, tiled=True
        ).astype(jnp.float32),
    )
    return (state_rows[None], down_share[None, None], up_share[None, None])


def solution(mesh):
    placed = (
        P("dp", "cand"),
        P("section", None),
        P("section", "dp", "cand"),
        P("section", None, "dp", None),
        P("section", "cand", "dp"),
        P("section", "cand", None),
        P("section", "cand", None, None),
        P("section", "cand", None, None),
        P("section", "cand"),
    )
    return jax.shard_map(
        shards,
        mesh=mesh,
        in_specs=placed,
        out_specs=(
            P("section", "dp", "cand"),
            P("section", "cand", None, "dp"),
            P("section", "cand", None, "dp"),
        ),
        check_vma=False,
    )
```

profile of v0, /device:TPU:29, one launch (start us, length us, event | category | flops | bytes accessed | tf_op | source)
XLA Modules:
  0.0 933.2 jit_solution(17415431154391329509)
XLA Ops:
  11.2 53.7 %all-gather.11.cloned.1.call-done = bf16[1,2,8192,128]{3,2,1,0:T(8,128)(2,1)} async-done(((bf16[1,2,1024,128]{3,2,1,0:T(8,128)(2,1)}), bf16[1,2,8192,128]{3,2,1,0:T(8,128)(2,1)}) %all-gather.11.cloned.1.call-update) | async-done | bytes 4194320 | tf_op jit(solution)/shard_map/all_gather | solution.py:94
  64.8 95.3 %all-gather.13.cloned.1.call-done = bf16[1,8192,512]{2,1,0:T(8,128)(2,1)} async-done(((bf16[1,1024,512]{2,1,0:T(8,128)(2,1)}), bf16[1,8192,512]{2,1,0:T(8,128)(2,1)}) %all-gather.13.cloned.1.call-update) | async-done | bytes 8388624 | tf_op jit(solution)/shard_map/all_gather | solution.py:93
  160.2 95.1 %all-gather.15.cloned.1.call-done = bf16[1,512,8192]{2,1,0:T(8,128)(2,1)} async-done(((bf16[1,512,1024]{2,1,0:T(8,128)(2,1)}), bf16[1,512,8192]{2,1,0:T(8,128)(2,1)}) %all-gather.15.cloned.1.call-update) | async-done | bytes 8388624 | tf_op jit(solution)/shard_map/all_gather | solution.py:95
  258.9 536.9 %while.23 = (s32[]{:T(128)}, bf16[64,1024]{1,0:T(8,128)(2,1)}, bf16[128,128]{1,0:T(8,128)(2,1)S(1)}, bf16[128,128]{1,0:T(8,128)(2,1)}, bf16[128,1024]{1,0:T(8,12...) while((s32[]{:T(128)}, bf16[64,1024]{1,0:T(8,128)(2,1)}, ...), condition=%wide.region_6.7_spmd.clone, body=%wide.region_0.6_spmd.clone.sunk | while | flops 1364615168 | bytes 46783588 | solution.py:184
  260.6 36.1 %all-gather.17.cloned.1.call-done = bf16[64,8192]{1,0:T(8,128)(2,1)} async-done(((bf16[64,1024]{1,0:T(8,128)(2,1)}), bf16[64,8192]{1,0:T(8,128)(2,1)}) %all-gather.17.cloned.1.call-update) | async-done | bytes 1048592 | tf_op jit(solution)/shard_map/while/body/eval_jaxpr/all_gather | solution.py:114
  299.9 6.1 convolution_convert_fusion.5
  306.0 49.2 %reduce-scatter.8.cloned.1.call-done = bf16[64,1024]{1,0:T(8,128)(2,1)} async-done(((bf16[64,8192]{1,0:T(8,128)(2,1)}), bf16[64,1024]{1,0:T(8,128)(2,1)}) %reduce-scatter.8.cloned.1.call-update) | async-done | bytes 131088 | tf_op jit(solution)/shard_map/while/body/eval_jaxpr/reduce_scatter | solution.py:166
  360.7 4.2 collective-permute-done
  366.7 37.9 %all-gather.17.cloned.1.call-done = bf16[64,8192]{1,0:T(8,128)(2,1)} async-done(((bf16[64,1024]{1,0:T(8,128)(2,1)}), bf16[64,8192]{1,0:T(8,128)(2,1)}) %all-gather.17.cloned.1.call-update) | async-done | bytes 1048592 | tf_op jit(solution)/shard_map/while/body/eval_jaxpr/all_gather | solution.py:114
  407.7 6.1 convolution_convert_fusion.5
  413.8 48.7 %reduce-scatter.8.cloned.1.call-done = bf16[64,1024]{1,0:T(8,128)(2,1)} async-done(((bf16[64,8192]{1,0:T(8,128)(2,1)}), bf16[64,1024]{1,0:T(8,128)(2,1)}) %reduce-scatter.8.cloned.1.call-update) | async-done | bytes 131088 | tf_op jit(solution)/shard_map/while/body/eval_jaxpr/reduce_scatter | solution.py:166
  467.9 4.7 collective-permute-done
  474.4 38.2 %all-gather.17.cloned.1.call-done = bf16[64,8192]{1,0:T(8,128)(2,1)} async-done(((bf16[64,1024]{1,0:T(8,128)(2,1)}), bf16[64,8192]{1,0:T(8,128)(2,1)}) %all-gather.17.cloned.1.call-update) | async-done | bytes 1048592 | tf_op jit(solution)/shard_map/while/body/eval_jaxpr/all_gather | solution.py:114
  515.7 6.1 convolution_convert_fusion.5
  521.8 50.7 %reduce-scatter.8.cloned.1.call-done = bf16[64,1024]{1,0:T(8,128)(2,1)} async-done(((bf16[64,8192]{1,0:T(8,128)(2,1)}), bf16[64,1024]{1,0:T(8,128)(2,1)}) %reduce-scatter.8.cloned.1.call-update) | async-done | bytes 131088 | tf_op jit(solution)/shard_map/while/body/eval_jaxpr/reduce_scatter | solution.py:166
  577.9 4.2 collective-permute-done
  583.9 37.9 %all-gather.17.cloned.1.call-done = bf16[64,8192]{1,0:T(8,128)(2,1)} async-done(((bf16[64,1024]{1,0:T(8,128)(2,1)}), bf16[64,8192]{1,0:T(8,128)(2,1)}) %all-gather.17.cloned.1.call-update) | async-done | bytes 1048592 | tf_op jit(solution)/shard_map/while/body/eval_jaxpr/all_gather | solution.py:114
  624.9 12.9 %conditional.3 = (bf16[64,512]{1,0:T(8,128)(2,1)S(1)}, bf16[128,128]{1,0:T(8,128)(2,1)S(1)}, bf16[128,128]{1,0:T(8,128)(2,1)}) conditional(s32[]{:T(128)} %convert_element_type.197, (bf16[128,128]{1,0:T(8,128)(2,1)S(1)}, bf16[128,128]{1,0:T(8,128)(2,1)}) %tuple.60, (bf16[2,8192,128]{2,1,0:T(8,128)(2,1)}, bf16[64,8192]{1,0:T(8,128)(2,1)S(1)}, ...), branch_computations={%region_2.2_spmd, %region_3.4_spmd} | conditional | flops 822632448 | bytes 17584966 | solution.py:160
  627.7 4.9 fusion.55
  637.8 6.1 convolution_convert_fusion.5
  643.9 37.7 %reduce-scatter.8.cloned.1.call-done = bf16[64,1024]{1,0:T(8,128)(2,1)} async-done(((bf16[64,8192]{1,0:T(8,128)(2,1)}), bf16[64,1024]{1,0:T(8,128)(2,1)}) %reduce-scatter.8.cloned.1.call-update) | async-done | bytes 131088 | tf_op jit(solution)/shard_map/while/body/eval_jaxpr/reduce_scatter | solution.py:166
  687.1 4.2 collective-permute-done
  693.1 37.9 %all-gather.17.cloned.1.call-done = bf16[64,8192]{1,0:T(8,128)(2,1)} async-done(((bf16[64,1024]{1,0:T(8,128)(2,1)}), bf16[64,8192]{1,0:T(8,128)(2,1)}) %all-gather.17.cloned.1.call-update) | async-done | bytes 1048592 | tf_op jit(solution)/shard_map/while/body/eval_jaxpr/all_gather | solution.py:114
  734.1 12.9 %conditional.3 = (bf16[64,512]{1,0:T(8,128)(2,1)S(1)}, bf16[128,128]{1,0:T(8,128)(2,1)S(1)}, bf16[128,128]{1,0:T(8,128)(2,1)}) conditional(s32[]{:T(128)} %convert_element_type.197, (bf16[128,128]{1,0:T(8,128)(2,1)S(1)}, bf16[128,128]{1,0:T(8,128)(2,1)}) %tuple.60, (bf16[2,8192,128]{2,1,0:T(8,128)(2,1)}, bf16[64,8192]{1,0:T(8,128)(2,1)S(1)}, ...), branch_computations={%region_2.2_spmd, %region_3.4_spmd} | conditional | flops 822632448 | bytes 17584966 | solution.py:160
  736.9 4.9 fusion.55
  747.0 6.1 convolution_convert_fusion.5
  753.1 33.0 %reduce-scatter.8.cloned.1.call-done = bf16[64,1024]{1,0:T(8,128)(2,1)} async-done(((bf16[64,8192]{1,0:T(8,128)(2,1)}), bf16[64,1024]{1,0:T(8,128)(2,1)}) %reduce-scatter.8.cloned.1.call-update) | async-done | bytes 131088 | tf_op jit(solution)/shard_map/while/body/eval_jaxpr/reduce_scatter | solution.py:166
  791.5 4.3 collective-permute-done
  801.6 37.6 %all-gather.9.cloned.1.call-done = bf16[128,8192]{1,0:T(8,128)(2,1)} async-done(((bf16[128,1024]{1,0:T(8,128)(2,1)}), bf16[128,8192]{1,0:T(8,128)(2,1)}) %all-gather.9.cloned.1.call-update) | async-done | bytes 2097168 | tf_op jit(solution)/shard_map/all_gather | solution.py:187
  845.3 4.9 convolution_convert_fusion.3
  850.2 32.0 %reduce-scatter.6.cloned.1.call-done = bf16[64,1024]{1,0:T(8,128)(2,1)} async-done(((bf16[64,8192]{1,0:T(8,128)(2,1)}), bf16[64,1024]{1,0:T(8,128)(2,1)}) %reduce-scatter.6.cloned.1.call-update) | async-done | bytes 131088 | tf_op jit(solution)/shard_map/reduce_scatter | solution.py:195
  883.8 41.2 %reduce-scatter.4.cloned.1.call-done = bf16[64,1024]{1,0:T(8,128)(2,1)} async-done(((bf16[64,8192]{1,0:T(8,128)(2,1)}), bf16[64,1024]{1,0:T(8,128)(2,1)}) %reduce-scatter.4.cloned.1.call-update) | async-done | bytes 131088 | tf_op jit(solution)/shard_map/reduce_scatter | solution.py:192
  (163 shorter events, 88.9 us)
Async XLA Ops:
  7.2 57.7 %all-gather.11.cloned.1.call-start = ((), (), s32[]{:S(2)}) async-start(), calls=%async_computation.6 | async-start | bytes 4718592 | tf_op jit(solution)/shard_map/all_gather | solution.py:94
  9.7 249.2 %copy-start.6 = (f32[1,8192]{1,0:T(1,128)S(1)}, f32[1,8192]{1,0:T(1,128)}, u32[]{:S(2)}) copy-start(f32[1,8192]{1,0:T(1,128)} %param.14) | copy-start | bytes 98308
  9.7 150.5 %all-gather.13.cloned.1.call-start = ((), (), s32[]{:S(2)}) async-start(), calls=%async_computation.7 | async-start | bytes 9437184 | tf_op jit(solution)/shard_map/all_gather | solution.py:93
  10.4 244.9 %all-gather.15.cloned.1.call-start = ((), (), s32[]{:S(2)}) async-start(), calls=%async_computation.8 | async-start | bytes 9437184 | tf_op jit(solution)/shard_map/all_gather | solution.py:95
  258.9 37.9 %all-gather.17.cloned.1.call-start = ((), (), s32[]{:S(2)}) async-start(), calls=%async_computation.9 | async-start | bytes 1179648 | tf_op jit(solution)/shard_map/while/body/eval_jaxpr/all_gather | solution.py:114
  260.6 94.6 %reduce-scatter.8.cloned.1.call-start = ((), (), s32[]{:S(2)}) async-start(), calls=%async_computation.10 | async-start | bytes 1179648 | tf_op jit(solution)/shard_map/while/body/eval_jaxpr/reduce_scatter | solution.py:166
  299.9 55.3 %copy-start.3 = (bf16[64,1024]{1,0:T(8,128)(2,1)S(1)}, bf16[64,1024]{1,0:T(8,128)(2,1)}, u32[]{:S(2)}) copy-start(bf16[64,1024]{1,0:T(8,128)(2,1)} %dynamic-slice_select_fusion.2) | copy-start | bytes 393220 | tf_op jit(solution)/shard_map/while
  306.0 52.2 %copy-start.1 = (bf16[64,8192]{1,0:T(8,128)(2,1)S(1)}, bf16[64,8192]{1,0:T(8,128)(2,1)}, u32[]{:S(2)}) copy-start(bf16[64,8192]{1,0:T(8,128)(2,1)} %all-gather.17.cloned.1.call-done) | copy-start | bytes 3145732 | tf_op jit(solution)/shard_map/while
  356.9 8.0 collective-permute-start
  364.9 39.6 %all-gather.17.cloned.1.call-start = ((), (), s32[]{:S(2)}) async-start(), calls=%async_computation.9 | async-start | bytes 1179648 | tf_op jit(solution)/shard_map/while/body/eval_jaxpr/all_gather | solution.py:114
  366.6 95.9 %reduce-scatter.8.cloned.1.call-start = ((), (), s32[]{:S(2)}) async-start(), calls=%async_computation.10 | async-start | bytes 1179648 | tf_op jit(solution)/shard_map/while/body/eval_jaxpr/reduce_scatter | solution.py:166
  407.7 54.8 %copy-start.3 = (bf16[64,1024]{1,0:T(8,128)(2,1)S(1)}, bf16[64,1024]{1,0:T(8,128)(2,1)}, u32[]{:S(2)}) copy-start(bf16[64,1024]{1,0:T(8,128)(2,1)} %dynamic-slice_select_fusion.2) | copy-start | bytes 393220 | tf_op jit(solution)/shard_map/while
  413.8 51.7 %copy-start.1 = (bf16[64,8192]{1,0:T(8,128)(2,1)S(1)}, bf16[64,8192]{1,0:T(8,128)(2,1)}, u32[]{:S(2)}) copy-start(bf16[64,8192]{1,0:T(8,128)(2,1)} %all-gather.17.cloned.1.call-done) | copy-start | bytes 3145732 | tf_op jit(solution)/shard_map/while
  464.2 8.5 collective-permute-start
  472.6 39.9 %all-gather.17.cloned.1.call-start = ((), (), s32[]{:S(2)}) async-start(), calls=%async_computation.9 | async-start | bytes 1179648 | tf_op jit(solution)/shard_map/while/body/eval_jaxpr/all_gather | solution.py:114
  474.3 98.1 %reduce-scatter.8.cloned.1.call-start = ((), (), s32[]{:S(2)}) async-start(), calls=%async_computation.10 | async-start | bytes 1179648 | tf_op jit(solution)/shard_map/while/body/eval_jaxpr/reduce_scatter | solution.py:166
  515.7 56.8 %copy-start.3 = (bf16[64,1024]{1,0:T(8,128)(2,1)S(1)}, bf16[64,1024]{1,0:T(8,128)(2,1)}, u32[]{:S(2)}) copy-start(bf16[64,1024]{1,0:T(8,128)(2,1)} %dynamic-slice_select_fusion.2) | copy-start | bytes 393220 | tf_op jit(solution)/shard_map/while
  521.8 53.7 %copy-start.1 = (bf16[64,8192]{1,0:T(8,128)(2,1)S(1)}, bf16[64,8192]{1,0:T(8,128)(2,1)}, u32[]{:S(2)}) copy-start(bf16[64,8192]{1,0:T(8,128)(2,1)} %all-gather.17.cloned.1.call-done) | copy-start | bytes 3145732 | tf_op jit(solution)/shard_map/while
  574.1 8.0 collective-permute-start
  582.1 39.6 %all-gather.17.cloned.1.call-start = ((), (), s32[]{:S(2)}) async-start(), calls=%async_computation.9 | async-start | bytes 1179648 | tf_op jit(solution)/shard_map/while/body/eval_jaxpr/all_gather | solution.py:114
  583.8 97.8 %reduce-scatter.8.cloned.1.call-start = ((), (), s32[]{:S(2)}) async-start(), calls=%async_computation.10 | async-start | bytes 1179648 | tf_op jit(solution)/shard_map/while/body/eval_jaxpr/reduce_scatter | solution.py:166
  637.8 43.8 %copy-start.3 = (bf16[64,1024]{1,0:T(8,128)(2,1)S(1)}, bf16[64,1024]{1,0:T(8,128)(2,1)}, u32[]{:S(2)}) copy-start(bf16[64,1024]{1,0:T(8,128)(2,1)} %dynamic-slice_select_fusion.2) | copy-start | bytes 393220 | tf_op jit(solution)/shard_map/while
  643.9 40.7 %copy-start.1 = (bf16[64,8192]{1,0:T(8,128)(2,1)S(1)}, bf16[64,8192]{1,0:T(8,128)(2,1)}, u32[]{:S(2)}) copy-start(bf16[64,8192]{1,0:T(8,128)(2,1)} %all-gather.17.cloned.1.call-done) | copy-start | bytes 3145732 | tf_op jit(solution)/shard_map/while
  683.3 8.0 collective-permute-start
  691.3 39.7 %all-gather.17.cloned.1.call-start = ((), (), s32[]{:S(2)}) async-start(), calls=%async_computation.9 | async-start | bytes 1179648 | tf_op jit(solution)/shard_map/while/body/eval_jaxpr/all_gather | solution.py:114
  693.0 93.1 %reduce-scatter.8.cloned.1.call-start = ((), (), s32[]{:S(2)}) async-start(), calls=%async_computation.10 | async-start | bytes 1179648 | tf_op jit(solution)/shard_map/while/body/eval_jaxpr/reduce_scatter | solution.py:166
  747.0 39.1 %copy-start.3 = (bf16[64,1024]{1,0:T(8,128)(2,1)S(1)}, bf16[64,1024]{1,0:T(8,128)(2,1)}, u32[]{:S(2)}) copy-start(bf16[64,1024]{1,0:T(8,128)(2,1)} %dynamic-slice_select_fusion.2) | copy-start | bytes 393220 | tf_op jit(solution)/shard_map/while
  787.8 8.0 collective-permute-start
  795.8 43.4 %all-gather.9.cloned.1.call-start = ((), (), s32[]{:S(2)}) async-start(), calls=%async_computation.3 | async-start | bytes 2359296 | tf_op jit(solution)/shard_map/all_gather | solution.py:187
  796.4 85.8 %reduce-scatter.6.cloned.1.call-start = ((), (), s32[]{:S(2)}) async-start(), calls=%async_computation.5 | async-start | bytes 1179648 | tf_op jit(solution)/shard_map/reduce_scatter | solution.py:195
  799.3 39.9 %copy-start.5 = (bf16[1,1,64,8192]{3,2,1,0:T(8,128)(2,1)S(1)}, bf16[1,1,64,8192]{3,2,1,0:T(8,128)(2,1)}, u32[]{:S(2)}) copy-start(bf16[1,1,64,8192]{3,2,1,0:T(8,128)(2,1)} %param.20) | copy-start | bytes 3145732
  845.3 79.8 %reduce-scatter.4.cloned.1.call-start = ((), (), s32[]{:S(2)}) async-start(), calls=%async_computation.4 | async-start | bytes 1179648 | tf_op jit(solution)/shard_map/reduce_scatter | solution.py:192
  (5 other events, 45.4 us)
Sparse Core Ops, SparseCore 0:
  9.8 54.9 all-gather.10
  66.6 93.5 all-gather.12
  162.0 93.2 all-gather.14
  261.8 34.9 all-gather.16
  306.2 49.0 reduce-scatter.7
  367.8 36.6 all-gather.16
  413.9 48.5 reduce-scatter.7
  475.8 36.6 all-gather.16
  521.9 50.4 reduce-scatter.7
  585.0 36.6 all-gather.16
  644.0 37.5 reduce-scatter.7
  694.2 36.7 all-gather.16
  753.2 32.8 reduce-scatter.7
  798.7 40.5 all-gather.8
  845.4 36.7 reduce-scatter.5
  884.6 40.4 reduce-scatter.3
where the time goes:
time: 942 us; the launch traced here: 933 us
  waiting for transfers between devices  786 us (83%)
  matrix products  63 us (7%)
  other arithmetic  50.9 us (5%)
  between operations  14.7 us (2%)
  local copies, waits for them, and re-layouts  11 us (1%)
    reduce_scatter x5, waiting for transfers between devices, turn(): lax.psum_scatter(projected.astype(jnp.bfloat16), 'cand', scatter_dimensio...  219 us
    all_gather x5, waiting for transfers between devices, turn(): features = lax.all_gather(arriving, 'cand', axis=1, tiled=True)  188 us
    all_gather x1, waiting for transfers between devices, shards(): lax.all_gather(query_weight[0], 'dp', axis=0, tiled=True)  95.3 us
    all_gather x1, waiting for transfers between devices, shards(): lax.all_gather(output_weight[0], 'dp', axis=1, tiled=True)  95.1 us
    all_gather x1, waiting for transfers between devices, shards(): lax.all_gather(selected, 'dp', axis=1, tiled=True)  53.7 us
    reduce_scatter x1, waiting for transfers between devices, shards(): lax.psum_scatter(down_total.astype(jnp.bfloat16), 'dp', scatter_dimension...  41.2 us
    all_gather x1, waiting for transfers between devices, shards(): targets = lax.all_gather(state_rows, 'cand', axis=1, tiled=True)  37.6 us
    reduce_scatter x1, waiting for transfers between devices, shards(): lax.psum_scatter(up_total.astype(jnp.bfloat16), 'dp', scatter_dimension=1...  32 us
  transfers between devices with their start and end apart: 21, of which 21 were waited for; matrix products, arithmetic and copies ran while one was open for 2% of the time, Pallas kernels for 0%

commit v1 on v0

v1 whole, which is shorter than its diff:
```python
import functools

import jax
import jax.numpy as jnp
import numpy as np
from jax import lax
from jax.experimental import pallas as pl
from jax.experimental.pallas import tpu as pltpu
from jax.sharding import PartitionSpec as P

HD = 128
LANES = 128
EPSILON = 1e-05
ROPE_BASE = 500000.0
MESH = pl.DeviceIdType.MESH
F32 = jnp.float32
BF16 = jnp.bfloat16


def dot_nt(a, b):
    return lax.dot_general(a, b, (((1,), (1,)), ((), ())), preferred_element_type=F32)


def dot_tn(a, b):
    return lax.dot_general(a, b, (((0,), (0,)), ((), ())), preferred_element_type=F32)


def rope_tables(tokens):
    half = HD // 2
    frequency = (ROPE_BASE ** (-np.arange(half, dtype=np.float64) / half)).astype(np.float32)
    angles = np.arange(tokens, dtype=np.float32)[:, None] * frequency[None, :]
    angles = angles.astype(np.float64)
    cosine, sine = np.cos(angles), np.sin(angles)
    full_cos = np.concatenate([cosine, cosine], axis=1).astype(np.float32)
    full_sin = np.concatenate([-sine, sine], axis=1).astype(np.float32)
    return full_cos, full_sin


def body(
    N,
    S,
    sharing,
    inputs,
    parent_gain,
    query_weight,
    key_value_weight,
    output_weight,
    candidate_gain,
    candidate_down,
    candidate_up,
    kept,
    cos_table,
    sin_table,
    states_out,
    down_out,
    up_out,
    x_buf,
    st_buf,
    sc_buf,
    p_buf,
    r_buf,
    a_own,
    a_buf,
    s_send,
    s_recv,
    part,
    w_qkv,
    w_out,
    w_down,
    w_up,
    pg,
    cg,
    cos_v,
    sin_v,
    bw_send,
    bw_recv,
    bw_all,
    y_buf,
    g_down,
    g_up,
    load_sem,
    in_send,
    in_recv,
    nx_send,
    nx_recv,
    ag_send,
    ag_recv,
    sg_send,
    sg_recv,
    p_send,
    p_recv,
    a_send,
    a_recv,
    rs_send,
    rs_recv,
    mate_send,
    mate_recv,
    y_send,
    y_recv,
    b_send,
    b_recv,
    c_send,
    c_recv,
):
    s = lax.axis_index("section")
    z = lax.axis_index("cand")
    i = lax.axis_index("dp")
    T, F = inputs.shape
    R = candidate_down.shape[2]
    D = N * F
    QW = query_weight.shape[2]
    heads = QW // HD
    KW = QW + 2 * HD
    piece = T // N
    half_rows = T // 2
    token_total = T * N
    middle = N // 2

    def wrap(index):
        return lax.rem(index + 2 * N, N)

    def rows(index):
        return pl.ds(pl.multiple_of(index * piece, piece), piece)

    def remote(source, target, send, recv, **device):
        return pltpu.make_async_remote_copy(
            src_ref=source,
            dst_ref=target,
            send_sem=send,
            recv_sem=recv,
            device_id=device,
            device_id_type=MESH,
        )

    def wait_bytes(ref, sem):
        pltpu.make_async_copy(ref, ref, sem).wait()

    features = pl.ds(pl.multiple_of(i * F, F), F)
    kv_columns = pl.ds(pl.multiple_of((z // sharing) * HD, HD), HD)
    loads = [
        (query_weight.at[0], w_qkv.at[:, pl.ds(0, QW)]),
        (key_value_weight.at[0, 0, :, kv_columns], w_qkv.at[:, pl.ds(QW, HD)]),
        (key_value_weight.at[0, 1, :, kv_columns], w_qkv.at[:, pl.ds(QW + HD, HD)]),
        (output_weight.at[0], w_out),
        (candidate_down.at[0, 0, :, features], w_down.at[pl.ds(0, R)]),
        (candidate_up.at[0, 0, :, features], w_up.at[pl.ds(0, R)]),
        (parent_gain.at[:, features], pg),
        (candidate_gain.at[0, :, features], cg),
        (cos_table, cos_v),
        (sin_table, sin_v),
    ]
    copies = [
        pltpu.make_async_copy(source, target, load_sem.at[k])
        for k, (source, target) in enumerate(loads)
    ]
    for copy in copies:
        copy.start()

    barrier = pltpu.get_barrier_semaphore()

    def greet(**device):
        pl.semaphore_signal(barrier, inc=1, device_id=device, device_id_type=MESH)

    diagonal = i == z
    greet(cand=wrap(z + 1))
    greet(cand=wrap(z - 1))
    for k in range(1, N):
        greet(dp=wrap(i + k))
    for w in range(N):

        @pl.when(jnp.logical_not(diagonal & (z == w)))
        def _(w=w):
            greet(dp=z, cand=w)
            greet(dp=w, cand=i)

    @pl.when(s > 0)
    def _():
        greet(section=s - 1)

    @pl.when(s < S - 1)
    def _():
        greet(section=s + 1)

    expected = (
        2
        + (N - 1)
        + 2 * N
        - 2 * diagonal.astype(jnp.int32)
        + (s > 0).astype(jnp.int32)
        + (s < S - 1).astype(jnp.int32)
    )
    pl.semaphore_wait(barrier, expected)

    def input_piece(w):
        source = inputs.at[pl.ds(w * piece, piece)]
        target = x_buf.at[w, rows(i)]
        return source, target

    @pl.when(s == 0)
    def _():
        for w in range(N):
            source, target = input_piece(w)
            own = diagonal & (z == w)

            @pl.when(own)
            def _(source=source, target=target):
                pltpu.make_async_copy(source, target, in_recv.at[0]).start()

            @pl.when(jnp.logical_not(own))
            def _(source=source, target=target, w=w):
                remote(source, target, in_send.at[w], in_recv.at[0], dp=z, cand=w).start()

    for copy in copies:
        copy.wait()
    w_down[pl.ds(R, LANES - R), :] = jnp.zeros((LANES - R, F), BF16)
    w_up[pl.ds(R, LANES - R), :] = jnp.zeros((LANES - R, F), BF16)
    w_down[pl.ds(0, R), :] = (w_down[pl.ds(0, R), :].astype(F32) * cg[...]).astype(BF16)

    def half(index):
        return pl.ds(index * half_rows, half_rows)

    def link(buffer, block, h, way, k, send, recv):
        place = buffer.at[block, half(h)]
        return remote(
            place, place, send.at[way, k], recv.at[way, k], cand=wrap(z + 1 - 2 * way)
        )

    def gather_own(buffer, h, send, recv):
        link(buffer, z, h, 0, h, send, recv).start()
        link(buffer, z, h, 1, 1 - h, send, recv).start()

    def gathered(k, way):
        distance = k // 2 + 1
        block = wrap(z - distance + 2 * distance * way)
        h = k % 2 if way == 0 else 1 - k % 2
        return block, h

    def gather_step(buffer, k, send, recv):
        for way in (0, 1):
            block, h = gathered(k, way)
            wait_bytes(buffer.at[block, half(h)], recv.at[way, k])
            if k + 2 <= N - 2:
                link(buffer, block, h, way, k + 2, send, recv).start()

    def gather_finish(buffer, send):
        for way in (0, 1):
            for k in range(N - 1):
                wait_bytes(buffer.at[0, half(0)], send.at[way, k])

    lane = lax.broadcasted_iota(jnp.int32, (T, LANES), 1)

    def project(block):
        values = x_buf[block]
        wide = values.astype(F32)
        scaled = (wide * pg[...]).astype(BF16)
        p_buf[block, :, pl.ds(0, KW)] = jnp.dot(
            scaled, w_qkv[...], preferred_element_type=F32
        ).astype(BF16)
        hidden = dot_nt(values, w_down[...])
        squares = jnp.sum(wide * wide, axis=-1, keepdims=True)
        coarse = squares.astype(BF16).astype(F32)
        extra = jnp.where(lane == R, coarse, jnp.where(lane == R + 1, squares - coarse, hidden))
        p_buf[block, :, pl.ds(KW, LANES)] = extra.astype(BF16)
        for k in range(1, N):
            t = wrap(i + k)
            remote(
                p_buf.at[block, rows(t)],
                r_buf.at[i, rows(block)],
                p_send.at[k],
                p_recv.at[k],
                dp=t,
            ).start()
        r_buf[i, rows(block), :] = p_buf[block, rows(i), :]

    @pl.when(s == 0)
    def _():
        wait_bytes(x_buf.at[z], in_recv.at[0])

    for h in (0, 1):

        @pl.when(s > 0)
        def _(h=h):
            wait_bytes(x_buf.at[z, half(h)], nx_recv.at[h])

        gather_own(x_buf, h, ag_send, ag_recv)
    project(z)
    for j in range(middle - 1):
        gather_step(x_buf, 2 * j, ag_send, ag_recv)
        gather_step(x_buf, 2 * j + 1, ag_send, ag_recv)
        project(wrap(z - j - 1))
        project(wrap(z + j + 1))
    gather_step(x_buf, N - 2, ag_send, ag_recv)
    project(wrap(z + middle))

    odd = lax.rem(s, 2) == 1

    def mate_copy(d):
        place = x_buf.at[wrap(z + d)]
        return remote(
            place, st_buf.at[wrap(z + d)], mate_send.at[d], mate_recv.at[d], section=s - 1
        )

    for k in range(1, N):
        wait_bytes(r_buf.at[wrap(i - k)], p_recv.at[k])

    def summed(b):
        total = r_buf[0, :, pl.ds(b * LANES, LANES)].astype(F32)
        for source in range(1, N):
            total += r_buf[source, :, pl.ds(b * LANES, LANES)].astype(F32)
        return total

    extra = summed(heads + 2)
    squares = extra[:, R : R + 1] + extra[:, R + 1 : R + 2]
    inverse = lax.rsqrt(squares / D + EPSILON)
    keep = (lax.broadcasted_iota(jnp.int32, (1, LANES), 1) < kept[0, 0]).astype(F32)
    hidden = extra * inverse * keep
    inverse_coarse = inverse.astype(BF16).astype(F32)
    a_own[:, pl.ds(QW, LANES)] = jnp.where(
        lane == R, inverse_coarse, jnp.where(lane == R + 1, inverse - inverse_coarse, hidden)
    ).astype(BF16)

    def rotated(matrix):
        return (matrix * cos_v[...] + pltpu.roll(matrix, HD // 2, 1) * sin_v[...]).astype(BF16)

    keys = rotated(summed(heads) * inverse)
    values = (summed(heads + 1) * inverse).astype(BF16)
    allowed = lax.broadcasted_iota(jnp.int32, (T, T), 1) <= lax.broadcasted_iota(
        jnp.int32, (T, T), 0
    )
    for h in range(heads):
        queries = rotated(summed(h) * inverse)
        scores = dot_nt(queries, keys) * HD ** (-0.5)
        raised = jnp.where(allowed, jnp.exp(scores), 0.0)
        weights = (raised / jnp.sum(raised, axis=-1, keepdims=True)).astype(BF16)
        a_own[:, pl.ds(h * HD, HD)] = jnp.dot(
            weights, values, preferred_element_type=F32
        ).astype(BF16)

    offsets = [middle]
    for m in range(middle - 1, 0, -1):
        offsets += [m, -m]
    offsets.append(0)
    for d, offset in enumerate(offsets):
        block = wrap(z + offset)
        for k in range(1, N):
            remote(
                a_own.at[rows(block)],
                a_buf.at[block, rows(i)],
                a_send.at[d],
                a_recv.at[d],
                dp=wrap(i + k),
            ).start()
        a_buf[block, rows(i), :] = a_own[rows(block), :]

    @pl.when(odd)
    def _():
        for d in range(1, N):
            mate_copy(d).start()

    def project_out(offset):
        d = offsets.index(offset)
        block = wrap(z + offset)
        wait_bytes(a_buf.at[block, pl.ds(0, T - piece)], a_recv.at[d])
        return jnp.dot(a_buf[block, :, pl.ds(0, QW)], w_out[...], preferred_element_type=F32)

    def emit(way, k, value):
        s_send[way, k] = value.astype(BF16)
        remote(
            s_send.at[way, k],
            s_recv.at[way, k],
            rs_send.at[way, k],
            rs_recv.at[way, k],
            cand=wrap(z + 1 - 2 * way),
        ).start()

    def got(way, k):
        wait_bytes(s_recv.at[way, k], rs_recv.at[way, k])
        return s_recv[way, k].astype(F32)

    first, second = half(0), half(1)
    part[0] = project_out(middle)
    emit(0, 0, part[0, first])
    emit(1, 0, part[0, second])
    for j, m in enumerate(range(middle - 1, 0, -1)):
        part[0] = project_out(m)
        part[1] = project_out(-m)
        if j == 0:
            emit(0, 1, part[0, second])
            emit(1, 1, part[1, first])
        else:
            emit(0, 2 * j + 1, got(0, 2 * j - 1) + part[0, second])
            emit(1, 2 * j + 1, got(1, 2 * j - 1) + part[1, first])
        emit(0, 2 * j + 2, got(0, 2 * j) + part[0, first])
        emit(1, 2 * j + 2, got(1, 2 * j) + part[1, second])
    part[0] = project_out(0)

    def next_copy(h):
        return remote(
            st_buf.at[z, half(h)], x_buf.at[z, half(h)], nx_send.at[h], nx_recv.at[h], section=s + 1
        )

    for h in (0, 1):
        update = part[0, half(h)] + got(0, N - 2 - h) + got(1, N - 3 + h)
        st_buf[z, half(h), :] = (x_buf[z, half(h), :].astype(F32) + update).astype(BF16)

        @pl.when(s < S - 1)
        def _(h=h):
            next_copy(h).start()

        @pl.when(odd)
        def _(h=h):
            gather_own(st_buf, h, sg_send, sg_recv)

    def state_piece(t):
        source = st_buf.at[z, pl.ds(t * piece, piece)]
        target = y_buf.at[rows(z)]
        return source, target

    for t in range(N):
        source, target = state_piece(t)
        own = diagonal & (i == t)

        @pl.when(own)
        def _(source=source, target=target):
            pltpu.make_async_copy(source, target, y_recv.at[0]).start()

        @pl.when(jnp.logical_not(own))
        def _(source=source, target=target, t=t):
            remote(source, target, y_send.at[t], y_recv.at[0], dp=t, cand=i).start()

    def candidate(block):
        hidden = a_buf[block, :, pl.ds(QW, LANES)]
        branch = jnp.dot(hidden, w_up[...], preferred_element_type=F32)
        difference = branch - (st_buf[block].astype(F32) - x_buf[block].astype(F32))
        scaled = (difference * (1.0 / token_total)).astype(BF16)
        sc_buf[block] = scaled
        backward = dot_nt(scaled, w_up[...]).astype(BF16)
        bw_send[block] = backward

        @pl.when(block == i)
        def _():
            bw_recv[i] = bw_send[block]

        @pl.when(block != i)
        def _():
            remote(
                bw_send.at[block], bw_recv.at[i], b_send.at[block], b_recv.at[0], dp=block
            ).start()

    candidate(z)
    for j in range(middle):
        last = j == middle - 1

        @pl.when(odd)
        def _(j=j, last=last):
            gather_step(st_buf, 2 * j, sg_send, sg_recv)
            if not last:
                gather_step(st_buf, 2 * j + 1, sg_send, sg_recv)

        @pl.when(jnp.logical_not(odd))
        def _(j=j, last=last):
            wait_bytes(st_buf.at[wrap(z + j + 1)], mate_recv.at[j + 1])
            if not last:
                wait_bytes(st_buf.at[wrap(z - j - 1)], mate_recv.at[N - j - 1])

        candidate(wrap(z + j + 1))
        if not last:
            candidate(wrap(z - j - 1))

    wait_bytes(bw_recv.at[pl.ds(0, N - 1)], b_recv.at[0])
    backward = bw_recv[0].astype(F32)
    for source in range(1, N):
        backward += bw_recv[source].astype(F32)
    own_extra = a_buf[i, :, pl.ds(QW, LANES)].astype(F32)
    own_inverse = own_extra[:, R : R + 1] + own_extra[:, R + 1 : R + 2]
    bw_all[i] = (backward * keep * own_inverse).astype(BF16)

    def spread(k):
        return remote(
            bw_all.at[i], bw_all.at[i], c_send.at[k], c_recv.at[0], dp=wrap(i + k)
        )

    for k in range(1, N):
        spread(k).start()

    hidden_all = a_buf[:, :, pl.ds(QW, LANES)].reshape(N * T, LANES)
    g_up[...] = dot_tn(hidden_all, sc_buf[...].reshape(N * T, F))
    up_copy = pltpu.make_async_copy(g_up.at[pl.ds(0, R)], up_out.at[0, 0], load_sem.at[0])
    up_copy.start()
    wait_bytes(y_buf, y_recv.at[0])
    y_copy = pltpu.make_async_copy(y_buf, states_out.at[0], load_sem.at[1])
    y_copy.start()

    wait_bytes(bw_all.at[pl.ds(0, N - 1)], c_recv.at[0])
    g_down[...] = (
        dot_tn(bw_all[...].reshape(N * T, LANES), x_buf[...].reshape(N * T, F)) * cg[...]
    )
    down_copy = pltpu.make_async_copy(g_down.at[pl.ds(0, R)], down_out.at[0, 0], load_sem.at[2])
    down_copy.start()

    @pl.when(s == 0)
    def _():
        for w in range(N):

            @pl.when(jnp.logical_not(diagonal & (z == w)))
            def _(w=w):
                wait_bytes(y_buf.at[pl.ds(0, piece)], in_send.at[w])

    gather_finish(x_buf, ag_send)
    for k in range(1, N):
        wait_bytes(r_buf.at[0], p_send.at[k])
        wait_bytes(bw_all.at[0], c_send.at[k])
    for d in range(N):
        wait_bytes(a_buf.at[0, pl.ds(0, T - piece)], a_send.at[d])
    for way in (0, 1):
        for k in range(N - 1):
            wait_bytes(s_send.at[way, k], rs_send.at[way, k])

    @pl.when(s < S - 1)
    def _():
        for h in (0, 1):
            wait_bytes(x_buf.at[0, half(h)], nx_send.at[h])

    @pl.when(odd)
    def _():
        gather_finish(st_buf, sg_send)
        for d in range(1, N):
            wait_bytes(x_buf.at[0], mate_send.at[d])

    for t in range(N):

        @pl.when(jnp.logical_not(diagonal & (i == t)))
        def _(t=t):
            wait_bytes(y_buf.at[pl.ds(0, piece)], y_send.at[t])

        @pl.when(i != t)
        def _(t=t):
            wait_bytes(bw_send.at[0], b_send.at[t])

    up_copy.wait()
    y_copy.wait()
    down_copy.wait()


def shards(
    inputs,
    parent_gain,
    query_weight,
    key_value_weight,
    output_weight,
    candidate_gain,
    candidate_down,
    candidate_up,
    kept_ranks,
):
    N = lax.axis_size("cand")
    S = lax.axis_size("section")
    T, F = inputs.shape
    R = candidate_down.shape[2]
    QW = query_weight.shape[2]
    KW = QW + 2 * HD
    half_rows = T // 2
    sharing = N // (key_value_weight.shape[3] // HD)
    cos_table, sin_table = rope_tables(T)
    anywhere = pl.BlockSpec(memory_space=pl.ANY)
    dma = pltpu.SemaphoreType.DMA
    return pl.pallas_call(
        functools.partial(body, N, S, sharing),
        out_shape=(
            jax.ShapeDtypeStruct((1, T, F), BF16),
            jax.ShapeDtypeStruct((1, 1, R, F), F32),
            jax.ShapeDtypeStruct((1, 1, R, F), F32),
        ),
        in_specs=[anywhere] * 8 + [pl.BlockSpec(memory_space=pltpu.SMEM)] + [anywhere] * 2,
        out_specs=(anywhere,) * 3,
        scratch_shapes=[
            pltpu.VMEM((N, T, F), BF16),
            pltpu.VMEM((N, T, F), BF16),
            pltpu.VMEM((N, T, F), BF16),
            pltpu.VMEM((N, T, KW + LANES), BF16),
            pltpu.VMEM((N, T, KW + LANES), BF16),
            pltpu.VMEM((T, QW + LANES), BF16),
            pltpu.VMEM((N, T, QW + LANES), BF16),
            pltpu.VMEM((2, N - 1, half_rows, F), BF16),
            pltpu.VMEM((2, N - 1, half_rows, F), BF16),
            pltpu.VMEM((2, T, F), F32),
            pltpu.VMEM((F, KW), BF16),
            pltpu.VMEM((QW, F), BF16),
            pltpu.VMEM((LANES, F), BF16),
            pltpu.VMEM((LANES, F), BF16),
            pltpu.VMEM((1, F), F32),
            pltpu.VMEM((1, F), F32),
            pltpu.VMEM((T, HD), F32),
            pltpu.VMEM((T, HD), F32),
            pltpu.VMEM((N, T, LANES), BF16),
            pltpu.VMEM((N, T, LANES), BF16),
            pltpu.VMEM((N, T, LANES), BF16),
            pltpu.VMEM((T, F), BF16),
            pltpu.VMEM((LANES, F), F32),
            pltpu.VMEM((LANES, F), F32),
            dma((10,)),
            dma((N,)),
            dma((1,)),
            dma((2,)),
            dma((2,)),
            dma((2, N - 1)),
            dma((2, N - 1)),
            dma((2, N - 1)),
            dma((2, N - 1)),
            dma((N,)),
            dma((N,)),
            dma((N,)),
            dma((N,)),
            dma((2, N - 1)),
            dma((2, N - 1)),
            dma((N,)),
            dma((N,)),
            dma((N,)),
            dma((1,)),
            dma((N,)),
            dma((1,)),
            dma((N,)),
            dma((1,)),
        ],
        compiler_params=pltpu.CompilerParams(
            collective_id=0, has_side_effects=True, vmem_limit_bytes=40 * 1024 * 1024
        ),
    )(
        inputs,
        parent_gain,
        query_weight,
        key_value_weight,
        output_weight,
        candidate_gain,
        candidate_down,
        candidate_up,
        kept_ranks,
        jnp.asarray(cos_table),
        jnp.asarray(sin_table),
    )


def solution(mesh):
    placed = (
        P("dp", "cand"),
        P("section", None),
        P("section", "dp", "cand"),
        P("section", None, "dp", None),
        P("section", "cand", "dp"),
        P("section", "cand", None),
        P("section", "cand", None, None),
        P("section", "cand", None, None),
        P("section", "cand"),
    )
    return jax.shard_map(
        shards,
        mesh=mesh,
        in_specs=placed,
        out_specs=(
            P("section", "dp", "cand"),
            P("section", "cand", None, "dp"),
            P("section", "cand", None, "dp"),
        ),
        check_vma=False,
    )
```

time: 942 us -> 274 us (0.29)
  waiting for transfers between devices: 786 us -> 0 us
  Pallas kernels: 0 us -> 259 us
  matrix products: 63 us -> 0 us
  other arithmetic: 50.9 us -> 0 us
  between operations: 14.7 us -> 1.31 us
    all_gather x9 -> x0, waiting for transfers between devices: 470 us -> none  [the longest x5 188 us: turn(): features = lax.all_gather(arriving, 'cand', axis=1, tiled=True)]
    reduce_scatter x7 -> x0, waiting for transfers between devices: 292 us -> none  [the longest x5 219 us: turn(): lax.psum_scatter(projected.astype(jnp.bfloat16), 'cand', scatter_dimensio...]
    pallas_call x0 -> x1, Pallas kernels: none -> 259 us  [shards(): pl.pallas_call(functools.partial(body, N, S, sharing), out_shape=(jax.Sha...]
    dot_general x19 -> x0, matrix products: 63 us -> none  [the longest x5 30.3 us: turn(): jnp.dot(attended, output_full, preferred_element_type=jnp.float32)]
    ppermute x5 -> x0, waiting for transfers between devices: 21.7 us -> none  [shifted(): return lax.ppermute(block, axis, route)]
    dynamic_update_slice x10 -> x0, other arithmetic: 20.7 us -> none  [place(): return lax.dynamic_update_slice_in_dim(buffer, chosen, offset, 0)]
    unnamed x12 -> x23, local copies, waits for them, and re-layouts: 2.86 us -> 12.7 us
    reduce_sum x6 -> x0, other arithmetic: 9.71 us -> none  [normed(): jnp.mean(wide * wide, axis=-1, keepdims=True) + epsilon]
  transfers between devices with their start and end apart: 21 -> 0, of which waited for: 21 -> 0; matrix products, arithmetic and copies ran while one was open for 2% -> 0% of each run, Pallas kernels for 0% -> 0%
where the time goes in v1:
time: 274 us; the launch traced here: 273 us
  Pallas kernels  259 us (95%)
  local copies, waits for them, and re-layouts  12.7 us (5%)
    pallas_call x1, Pallas kernels, shards(): pl.pallas_call(functools.partial(body, N, S, sharing), out_shape=(jax.Sha...  259 us
    unnamed x23, local copies, waits for them, and re-layouts  12.7 us

profile of v1, /device:TPU:29, one launch (start us, length us, event | category | flops | bytes accessed | tf_op | source)
XLA Modules:
  0.0 273.2 jit_solution(9637951274504097176)
XLA Ops:
  1.3 0.0 copy-start
  1.3 1.6 copy-done
  2.9 0.0 copy-start.1
  2.9 1.2 copy-done.1
  4.1 0.0 copy-start.2
  4.1 1.2 copy-done.2
  5.3 0.0 copy-start.3
  5.3 1.2 copy-done.3
  6.5 0.0 copy-start.4
  6.5 1.2 copy-done.4
  7.8 0.0 copy-start.5
  7.8 0.9 copy-done.5
  8.7 0.0 copy-start.6
  8.7 0.8 copy-done.6
  9.6 0.0 copy-start.7
  9.6 0.8 copy-done.7
  10.4 0.0 copy-start.8
  10.4 0.8 copy-done.8
  11.2 0.0 copy-start.9
  11.2 0.8 copy-done.9
  11.9 259.2 %shard_map.130 = (bf16[1,128,1024]{2,1,0:T(8,128)(2,1)S(1)}, f32[1,1,64,1024]{3,2,1,0:T(8,128)S(1)}, f32[1,1,64,1024]{3,2,1,0:T(8,128)S(1)}) custom-call(bf16[128,1024]{1,0:T(8,128)(2,1)S(1)} %copy-done.5, f32[1,8192]{1,0:T(1,128)S(1)} %copy-done.8, bf16[1,1024,512]{2,1,0:T(8,128)(2,1)S(1)} %copy-done.1, bf16[1,2,1024,512]{3,2,1,0:T(8,128)(2,1)S(1)} %copy-done, ...), custom_call_target="tpu_custom_call" | custom-call | tf_op jit(solution)/shard_map/pallas_call | solution.py:567
  271.1 0.7 copy.18
  271.8 0.7 copy.19
  272.5 0.7 copy.20
Async XLA Ops:
  1.3 1.6 copy-start
  2.9 1.2 copy-start.1
  4.1 1.2 copy-start.2
  5.3 1.2 copy-start.3
  6.5 1.2 copy-start.4
  7.8 0.9 copy-start.5
  8.7 0.8 copy-start.6
  9.6 0.8 copy-start.7
  10.4 0.8 copy-start.8
  11.2 0.8 copy-start.9

commit v2 on v1

v2 whole, which is shorter than its diff:
```python
import functools

import jax
import jax.numpy as jnp
import numpy as np
from jax import lax
from jax.experimental import pallas as pl
from jax.experimental.pallas import tpu as pltpu
from jax.sharding import PartitionSpec as P

HD = 128
LANES = 128
PIECES = 4
EPSILON = 1e-05
ROPE_BASE = 500000.0
MESH = pl.DeviceIdType.MESH
F32 = jnp.float32
BF16 = jnp.bfloat16


def dot_nt(a, b):
    return lax.dot_general(a, b, (((1,), (1,)), ((), ())), preferred_element_type=F32)


def dot_tn(a, b):
    return lax.dot_general(a, b, (((0,), (0,)), ((), ())), preferred_element_type=F32)


def rope_tables(tokens):
    half = HD // 2
    frequency = (ROPE_BASE ** (-np.arange(half, dtype=np.float64) / half)).astype(np.float32)
    angles = np.arange(tokens, dtype=np.float32)[:, None] * frequency[None, :]
    angles = angles.astype(np.float64)
    cosine, sine = np.cos(angles), np.sin(angles)
    full_cos = np.concatenate([cosine, cosine], axis=1).astype(np.float32)
    full_sin = np.concatenate([-sine, sine], axis=1).astype(np.float32)
    return full_cos, full_sin


def body(
    N,
    S,
    sharing,
    inputs,
    parent_gain,
    query_weight,
    key_value_weight,
    output_weight,
    candidate_gain,
    candidate_down,
    candidate_up,
    kept,
    cos_table,
    sin_table,
    states_out,
    down_out,
    up_out,
    x_buf,
    st_buf,
    sc_buf,
    p_buf,
    r_buf,
    a_own,
    a_buf,
    s_send,
    s_recv,
    part,
    w_qkv,
    w_out,
    w_down,
    w_up,
    pg,
    cg,
    cos_v,
    sin_v,
    bw_send,
    bw_recv,
    bw_all,
    y_buf,
    g_down,
    g_up,
    load_sem,
    in_send,
    in_recv,
    nx_send,
    nx_recv,
    ag_send,
    ag_recv,
    sg_send,
    sg_recv,
    p_send,
    p_recv,
    a_send,
    a_recv,
    rs_send,
    rs_recv,
    mate_send,
    mate_recv,
    y_send,
    y_recv,
    b_send,
    b_recv,
    c_send,
    c_recv,
):
    s = lax.axis_index("section")
    z = lax.axis_index("cand")
    i = lax.axis_index("dp")
    T, F = inputs.shape
    R = candidate_down.shape[2]
    D = N * F
    QW = query_weight.shape[2]
    heads = QW // HD
    KW = QW + 2 * HD
    piece = T // N
    token_total = T * N
    middle = N // 2

    def wrap(index):
        return lax.rem(index + 2 * N, N)

    def rows(index):
        return pl.ds(pl.multiple_of(index * piece, piece), piece)

    def remote(source, target, send, recv, **device):
        return pltpu.make_async_remote_copy(
            src_ref=source,
            dst_ref=target,
            send_sem=send,
            recv_sem=recv,
            device_id=device,
            device_id_type=MESH,
        )

    def wait_bytes(ref, sem):
        pltpu.make_async_copy(ref, ref, sem).wait()

    features = pl.ds(pl.multiple_of(i * F, F), F)
    kv_columns = pl.ds(pl.multiple_of((z // sharing) * HD, HD), HD)
    loads = [
        (query_weight.at[0], w_qkv.at[:, pl.ds(0, QW)]),
        (key_value_weight.at[0, 0, :, kv_columns], w_qkv.at[:, pl.ds(QW, HD)]),
        (key_value_weight.at[0, 1, :, kv_columns], w_qkv.at[:, pl.ds(QW + HD, HD)]),
        (output_weight.at[0], w_out),
        (candidate_down.at[0, 0, :, features], w_down.at[pl.ds(0, R)]),
        (candidate_up.at[0, 0, :, features], w_up.at[pl.ds(0, R)]),
        (parent_gain.at[:, features], pg),
        (candidate_gain.at[0, :, features], cg),
        (cos_table, cos_v),
        (sin_table, sin_v),
    ]
    copies = [
        pltpu.make_async_copy(source, target, load_sem.at[k])
        for k, (source, target) in enumerate(loads)
    ]
    for copy in copies:
        copy.start()

    barrier = pltpu.get_barrier_semaphore()

    def greet(**device):
        pl.semaphore_signal(barrier, inc=1, device_id=device, device_id_type=MESH)

    diagonal = i == z
    odd = lax.rem(s, 2) == 1
    greet(cand=wrap(z + 1))
    greet(cand=wrap(z - 1))
    for k in range(1, N):
        greet(dp=wrap(i + k))
    for w in range(N):

        @pl.when(jnp.logical_not(diagonal & (z == w)))
        def _(w=w):
            greet(dp=z, cand=w)
            greet(dp=w, cand=i)

    @pl.when(s > 0)
    def _():
        greet(section=s - 1)

    @pl.when(s < S - 1)
    def _():
        greet(section=s + 1)

    mate = s + 1 - 2 * lax.rem(s, 2)
    greet(section=mate, cand=wrap(z + 1))
    greet(section=mate, cand=wrap(z - 1))

    expected = (
        4
        + (N - 1)
        + 2 * N
        - 2 * diagonal.astype(jnp.int32)
        + (s > 0).astype(jnp.int32)
        + (s < S - 1).astype(jnp.int32)
    )
    pl.semaphore_wait(barrier, expected)

    pieces = PIECES
    messages = (N - 1) * pieces // 2
    piece_rows = T // pieces

    def part_rows(q):
        return pl.ds(q * piece_rows, piece_rows)

    def piece_of(way, k):
        return k % pieces if way == 0 else pieces - 1 - k % pieces

    def toward(way):
        return wrap(z + 1 - 2 * way)

    def send_input():
        for w in range(N):
            source = inputs.at[pl.ds(w * piece, piece)]
            target = x_buf.at[w, rows(i)]
            own = diagonal & (z == w)

            @pl.when(own)
            def _(source=source, target=target):
                pltpu.make_async_copy(source, target, in_recv.at[0]).start()

            @pl.when(jnp.logical_not(own))
            def _(source=source, target=target, w=w):
                remote(source, target, in_send.at[0], in_recv.at[0], dp=z, cand=w).start()

    def wait_pieces_sent(sem):
        @pl.when(diagonal)
        def _():
            wait_bytes(y_buf.at[pl.ds(0, T - piece)], sem)

        @pl.when(jnp.logical_not(diagonal))
        def _():
            wait_bytes(y_buf, sem)

    def prepare():
        for copy in copies:
            copy.wait()
        w_down[pl.ds(R, LANES - R), :] = jnp.zeros((LANES - R, F), BF16)
        w_up[pl.ds(R, LANES - R), :] = jnp.zeros((LANES - R, F), BF16)
        w_down[pl.ds(0, R), :] = (w_down[pl.ds(0, R), :].astype(F32) * cg[...]).astype(BF16)

    def forward(buffer, block, way, k, send, recv):
        place = buffer.at[block, part_rows(piece_of(way, k))]
        remote(place, place, send.at[0], recv.at[way, k], cand=toward(way)).start()

    def gather_step(buffer, k, send, recv):
        distance = k // pieces + 1
        for way in (0, 1):
            block = wrap(z - distance + 2 * distance * way)
            wait_bytes(buffer.at[block, part_rows(piece_of(way, k))], recv.at[way, k])
            if k + pieces < messages:
                forward(buffer, block, way, k + pieces, send, recv)

    lane = lax.broadcasted_iota(jnp.int32, (T, LANES), 1)
    keep = (lax.broadcasted_iota(jnp.int32, (1, LANES), 1) < kept[0, 0]).astype(F32)

    def project(block):
        values = x_buf[block]
        wide = values.astype(F32)
        scaled = (wide * pg[...]).astype(BF16)
        p_buf[block, :, pl.ds(0, KW)] = jnp.dot(
            scaled, w_qkv[...], preferred_element_type=F32
        ).astype(BF16)
        hidden = dot_nt(values, w_down[...])
        squares = jnp.sum(wide * wide, axis=-1, keepdims=True)
        coarse = squares.astype(BF16).astype(F32)
        extra = jnp.where(lane == R, coarse, jnp.where(lane == R + 1, squares - coarse, hidden))
        p_buf[block, :, pl.ds(KW, LANES)] = extra.astype(BF16)
        for k in range(1, N):
            t = wrap(i + k)
            remote(
                p_buf.at[block, rows(t)],
                r_buf.at[i, rows(block)],
                p_send.at[0],
                p_recv.at[0],
                dp=t,
            ).start()
        r_buf[i, rows(block), :] = p_buf[block, rows(i), :]

    def gather_and_project():
        @pl.when(s == 0)
        def _():
            wait_bytes(x_buf.at[z], in_recv.at[0])

        for q in range(pieces):

            @pl.when(s > 0)
            def _(q=q):
                wait_bytes(x_buf.at[z, part_rows(q)], nx_recv.at[q])

            @pl.when(jnp.logical_not(odd))
            def _(q=q):
                forward(x_buf, z, 0, q, ag_send, ag_recv)
                forward(x_buf, z, 1, pieces - 1 - q, ag_send, ag_recv)

        project(z)
        for j in range(middle):
            for k in range(j * pieces, min((j + 1) * pieces, messages)):
                gather_step(x_buf, k, ag_send, ag_recv)
            project(wrap(z + j + 1))
            if j < middle - 1:
                project(wrap(z - j - 1))

    def summed(b):
        total = r_buf[0, :, pl.ds(b * LANES, LANES)].astype(F32)
        for source in range(1, N):
            total += r_buf[source, :, pl.ds(b * LANES, LANES)].astype(F32)
        return total

    def rotated(matrix):
        return (matrix * cos_v[...] + pltpu.roll(matrix, HD // 2, 1) * sin_v[...]).astype(BF16)

    offsets = [middle]
    for m in range(middle - 1, 0, -1):
        offsets += [m, -m]
    offsets.append(0)

    def attention():
        wait_bytes(r_buf.at[pl.ds(0, N - 1)], p_recv.at[0])
        extra = summed(heads + 2)
        squares = extra[:, R : R + 1] + extra[:, R + 1 : R + 2]
        inverse = lax.rsqrt(squares / D + EPSILON)
        hidden = extra * inverse * keep
        inverse_coarse = inverse.astype(BF16).astype(F32)
        a_own[:, pl.ds(QW, LANES)] = jnp.where(
            lane == R, inverse_coarse, jnp.where(lane == R + 1, inverse - inverse_coarse, hidden)
        ).astype(BF16)
        keys = rotated(summed(heads) * inverse)
        values = (summed(heads + 1) * inverse).astype(BF16)
        allowed = lax.broadcasted_iota(jnp.int32, (T, T), 1) <= lax.broadcasted_iota(
            jnp.int32, (T, T), 0
        )
        for h in range(heads):
            queries = rotated(summed(h) * inverse)
            scores = dot_nt(queries, keys) * HD ** (-0.5)
            raised = jnp.where(allowed, jnp.exp(scores), 0.0)
            weights = (raised / jnp.sum(raised, axis=-1, keepdims=True)).astype(BF16)
            a_own[:, pl.ds(h * HD, HD)] = jnp.dot(
                weights, values, preferred_element_type=F32
            ).astype(BF16)
        for d, offset in enumerate(offsets):
            block = wrap(z + offset)
            for k in range(1, N):
                remote(
                    a_own.at[rows(block)],
                    a_buf.at[block, rows(i)],
                    a_send.at[0],
                    a_recv.at[d],
                    dp=wrap(i + k),
                ).start()
            a_buf[block, rows(i), :] = a_own[rows(block), :]

    def project_out(slot, offset):
        block = wrap(z + offset)
        wait_bytes(a_buf.at[block, pl.ds(0, T - piece)], a_recv.at[offsets.index(offset)])
        part[slot] = jnp.dot(
            a_buf[block, :, pl.ds(0, QW)], w_out[...], preferred_element_type=F32
        )

    def got(way, k):
        wait_bytes(s_recv.at[way, k], rs_recv.at[way, k])
        return s_recv[way, k].astype(F32)

    def emit(slot, way, k):
        value = part[slot, part_rows(piece_of(way, k)), :]
        if k >= pieces:
            value += got(way, k - pieces)
        s_send[way, k] = value.astype(BF16)
        remote(
            s_send.at[way, k],
            s_recv.at[way, k],
            rs_send.at[0],
            rs_recv.at[way, k],
            cand=toward(way),
        ).start()

    def output():
        project_out(0, middle)
        for k in range(pieces // 2):
            emit(0, 0, k)
            emit(0, 1, k)
        for j, m in enumerate(range(middle - 1, 0, -1)):
            project_out(0, m)
            project_out(1, -m)
            for k in range(pieces // 2 + j * pieces, pieces // 2 + (j + 1) * pieces):
                emit(0, 0, k)
                emit(1, 1, k)
        project_out(0, 0)
        part[0] += x_buf[z].astype(F32)
        for k in range(messages - pieces, messages):
            for way in (0, 1):
                place = part_rows(piece_of(way, k))
                total = part[0, place, :] + got(way, k)
                part[0, place, :] = total

    def hand_over():
        st_buf[z] = part[0].astype(BF16)

        @pl.when(jnp.logical_not(odd))
        def _():
            for k in range(pieces):
                for way in (0, 1):
                    place = part_rows(piece_of(way, k))
                    remote(
                        st_buf.at[z, place],
                        x_buf.at[z, place],
                        nx_send.at[0],
                        ag_recv.at[way, k],
                        section=s + 1,
                        cand=toward(way),
                    ).start()

        @pl.when(s < S - 1)
        def _():
            for q in range(pieces):
                remote(
                    st_buf.at[z, part_rows(q)],
                    x_buf.at[z, part_rows(q)],
                    nx_send.at[0],
                    nx_recv.at[q],
                    section=s + 1,
                ).start()

        @pl.when(odd)
        def _():
            for q in range(pieces):
                forward(st_buf, z, 0, q, sg_send, sg_recv)
                forward(st_buf, z, 1, pieces - 1 - q, sg_send, sg_recv)
            for d in range(1, N):
                place = x_buf.at[wrap(z + d)]
                remote(
                    place,
                    st_buf.at[wrap(z + d)],
                    mate_send.at[0],
                    mate_recv.at[d],
                    section=s - 1,
                ).start()

        for t in range(N):
            source = st_buf.at[z, pl.ds(t * piece, piece)]
            target = y_buf.at[rows(z)]
            own = diagonal & (i == t)

            @pl.when(own)
            def _(source=source, target=target):
                pltpu.make_async_copy(source, target, y_recv.at[0]).start()

            @pl.when(jnp.logical_not(own))
            def _(source=source, target=target, t=t):
                remote(source, target, y_send.at[0], y_recv.at[0], dp=t, cand=i).start()

    def candidate(block):
        hidden = a_buf[block, :, pl.ds(QW, LANES)]
        branch = jnp.dot(hidden, w_up[...], preferred_element_type=F32)
        difference = branch - (st_buf[block].astype(F32) - x_buf[block].astype(F32))
        scaled = (difference * (1.0 / token_total)).astype(BF16)
        sc_buf[block] = scaled
        bw_send[block] = dot_nt(scaled, w_up[...]).astype(BF16)

        @pl.when(block == i)
        def _():
            bw_recv[i] = bw_send[block]

        @pl.when(block != i)
        def _():
            remote(
                bw_send.at[block], bw_recv.at[i], b_send.at[0], b_recv.at[0], dp=block
            ).start()

    def candidates():
        candidate(z)
        for j in range(middle):
            last = j == middle - 1

            @pl.when(odd)
            def _(j=j):
                for k in range(j * pieces, min((j + 1) * pieces, messages)):
                    gather_step(st_buf, k, sg_send, sg_recv)

            @pl.when(jnp.logical_not(odd))
            def _(j=j, last=last):
                wait_bytes(st_buf.at[wrap(z + j + 1)], mate_recv.at[j + 1])
                if not last:
                    wait_bytes(st_buf.at[wrap(z - j - 1)], mate_recv.at[N - j - 1])

            candidate(wrap(z + j + 1))
            if not last:
                candidate(wrap(z - j - 1))

    def gradients():
        wait_bytes(bw_recv.at[pl.ds(0, N - 1)], b_recv.at[0])
        backward = bw_recv[0].astype(F32)
        for source in range(1, N):
            backward += bw_recv[source].astype(F32)
        own_extra = a_buf[i, :, pl.ds(QW, LANES)].astype(F32)
        own_inverse = own_extra[:, R : R + 1] + own_extra[:, R + 1 : R + 2]
        bw_all[i] = (backward * keep * own_inverse).astype(BF16)
        for k in range(1, N):
            remote(
                bw_all.at[i], bw_all.at[i], c_send.at[0], c_recv.at[0], dp=wrap(i + k)
            ).start()

        hidden_all = a_buf[:, :, pl.ds(QW, LANES)].reshape(N * T, LANES)
        g_up[...] = dot_tn(hidden_all, sc_buf[...].reshape(N * T, F))
        up_copy = pltpu.make_async_copy(g_up.at[pl.ds(0, R)], up_out.at[0, 0], load_sem.at[0])
        up_copy.start()
        wait_bytes(y_buf, y_recv.at[0])
        y_copy = pltpu.make_async_copy(y_buf, states_out.at[0], load_sem.at[1])
        y_copy.start()

        wait_bytes(bw_all.at[pl.ds(0, N - 1)], c_recv.at[0])
        g_down[...] = (
            dot_tn(bw_all[...].reshape(N * T, LANES), x_buf[...].reshape(N * T, F)) * cg[...]
        )
        down_copy = pltpu.make_async_copy(
            g_down.at[pl.ds(0, R)], down_out.at[0, 0], load_sem.at[2]
        )
        down_copy.start()
        up_copy.wait()
        y_copy.wait()
        down_copy.wait()

    def drain():
        @pl.when(s == 0)
        def _():
            wait_pieces_sent(in_send.at[0])

        others = pl.ds(0, N - 1)

        @pl.when(jnp.logical_not(odd))
        def _():
            wait_bytes(x_buf.at[others], ag_send.at[0])
            wait_bytes(x_buf.at[pl.ds(0, 3)], nx_send.at[0])

        @pl.when(odd)
        def _():
            wait_bytes(x_buf.at[pl.ds(0, N - 3)], ag_send.at[0])
            wait_bytes(st_buf.at[others], sg_send.at[0])
            wait_bytes(st_buf.at[others], mate_send.at[0])

            @pl.when(s < S - 1)
            def _():
                wait_bytes(x_buf.at[0], nx_send.at[0])

        wait_bytes(p_buf.at[others], p_send.at[0])
        wait_bytes(a_buf.at[others], a_send.at[0])
        wait_bytes(s_send, rs_send.at[0])
        wait_pieces_sent(y_send.at[0])
        wait_bytes(bw_send.at[others], b_send.at[0])
        wait_bytes(bw_all.at[others], c_send.at[0])

    @pl.when(s == 0)
    def _():
        send_input()

    prepare()
    gather_and_project()
    attention()
    output()
    hand_over()
    candidates()
    gradients()
    drain()


def shards(
    inputs,
    parent_gain,
    query_weight,
    key_value_weight,
    output_weight,
    candidate_gain,
    candidate_down,
    candidate_up,
    kept_ranks,
):
    N = lax.axis_size("cand")
    S = lax.axis_size("section")
    T, F = inputs.shape
    R = candidate_down.shape[2]
    QW = query_weight.shape[2]
    KW = QW + 2 * HD
    pieces = PIECES
    messages = (N - 1) * pieces // 2
    sharing = N // (key_value_weight.shape[3] // HD)
    cos_table, sin_table = rope_tables(T)
    anywhere = pl.BlockSpec(memory_space=pl.ANY)
    dma = pltpu.SemaphoreType.DMA
    return pl.pallas_call(
        functools.partial(body, N, S, sharing),
        out_shape=(
            jax.ShapeDtypeStruct((1, T, F), BF16),
            jax.ShapeDtypeStruct((1, 1, R, F), F32),
            jax.ShapeDtypeStruct((1, 1, R, F), F32),
        ),
        in_specs=[anywhere] * 8 + [pl.BlockSpec(memory_space=pltpu.SMEM)] + [anywhere] * 2,
        out_specs=(anywhere,) * 3,
        scratch_shapes=[
            pltpu.VMEM((N, T, F), BF16),
            pltpu.VMEM((N, T, F), BF16),
            pltpu.VMEM((N, T, F), BF16),
            pltpu.VMEM((N, T, KW + LANES), BF16),
            pltpu.VMEM((N, T, KW + LANES), BF16),
            pltpu.VMEM((T, QW + LANES), BF16),
            pltpu.VMEM((N, T, QW + LANES), BF16),
            pltpu.VMEM((2, messages, T // pieces, F), BF16),
            pltpu.VMEM((2, messages, T // pieces, F), BF16),
            pltpu.VMEM((2, T, F), F32),
            pltpu.VMEM((F, KW), BF16),
            pltpu.VMEM((QW, F), BF16),
            pltpu.VMEM((LANES, F), BF16),
            pltpu.VMEM((LANES, F), BF16),
            pltpu.VMEM((1, F), F32),
            pltpu.VMEM((1, F), F32),
            pltpu.VMEM((T, HD), F32),
            pltpu.VMEM((T, HD), F32),
            pltpu.VMEM((N, T, LANES), BF16),
            pltpu.VMEM((N, T, LANES), BF16),
            pltpu.VMEM((N, T, LANES), BF16),
            pltpu.VMEM((T, F), BF16),
            pltpu.VMEM((LANES, F), F32),
            pltpu.VMEM((LANES, F), F32),
            dma((10,)),
            dma((1,)),
            dma((1,)),
            dma((1,)),
            dma((pieces,)),
            dma((1,)),
            dma((2, messages)),
            dma((1,)),
            dma((2, messages)),
            dma((1,)),
            dma((1,)),
            dma((1,)),
            dma((N,)),
            dma((1,)),
            dma((2, messages)),
            dma((1,)),
            dma((N,)),
            dma((1,)),
            dma((1,)),
            dma((1,)),
            dma((1,)),
            dma((1,)),
            dma((1,)),
        ],
        compiler_params=pltpu.CompilerParams(
            collective_id=0, has_side_effects=True, vmem_limit_bytes=56 * 1024 * 1024
        ),
    )(
        inputs,
        parent_gain,
        query_weight,
        key_value_weight,
        output_weight,
        candidate_gain,
        candidate_down,
        candidate_up,
        kept_ranks,
        jnp.asarray(cos_table),
        jnp.asarray(sin_table),
    )


def solution(mesh):
    placed = (
        P("dp", "cand"),
        P("section", None),
        P("section", "dp", "cand"),
        P("section", None, "dp", None),
        P("section", "cand", "dp"),
        P("section", "cand", None),
        P("section", "cand", None, None),
        P("section", "cand", None, None),
        P("section", "cand"),
    )
    return jax.shard_map(
        shards,
        mesh=mesh,
        in_specs=placed,
        out_specs=(
            P("section", "dp", "cand"),
            P("section", "cand", None, "dp"),
            P("section", "cand", None, "dp"),
        ),
        check_vma=False,
    )
```

time: 274 us -> 252 us (0.920)
  Pallas kernels: 259 us -> 246 us
  local copies, waits for them, and re-layouts: 12.7 us -> 5.01 us
    pallas_call x1, Pallas kernels: 259 us -> 246 us  [shards(): pl.pallas_call(functools.partial(body, N, S, sharing), out_shape=(jax.Sha...]
    unnamed x23 -> x3, local copies, waits for them, and re-layouts: 12.7 us -> 5.01 us
where the time goes in v2:
time: 252 us
  Pallas kernels  246 us (98%)
  local copies, waits for them, and re-layouts  5.01 us (2%)
    pallas_call x1, Pallas kernels, shards(): pl.pallas_call(functools.partial(body, N, S, sharing), out_shape=(jax.Sha...  246 us

profile of v2, /device:TPU:29, one launch (start us, length us, event | category | flops | bytes accessed | tf_op | source)
XLA Modules:
  0.0 252.1 jit_solution(15103937022424690611)
XLA Ops:
  1.3 245.8 %shard_map.130 = (bf16[1,128,1024]{2,1,0:T(8,128)(2,1)}, f32[1,1,64,1024]{3,2,1,0:T(8,128)}, f32[1,1,64,1024]{3,2,1,0:T(8,128)}) custom-call(bf16[128,1024]{1,0:T(8,128)(2,1)} %inputs.1, f32[1,8192]{1,0:T(1,128)} %parent_gain.1, bf16[1,1024,512]{2,1,0:T(8,128)(2,1)} %query_weight.1, bf16[1,2,1024,512]{3,2,1,0:T(8,128)(2,1)} %key_value_weight.1, ...), custom_call_target="tpu_custom_call" | custom-call | tf_op jit(solution)/shard_map/pallas_call | solution.py:589
  247.1 1.7 copy.18
  248.8 1.7 copy.19
  250.4 1.7 copy.20

commit v3 on v2

--- a/solution.py
+++ b/solution.py
@@ -239,17 +239,42 @@
         w_up[pl.ds(R, LANES - R), :] = jnp.zeros((LANES - R, F), BF16)
         w_down[pl.ds(0, R), :] = (w_down[pl.ds(0, R), :].astype(F32) * cg[...]).astype(BF16)
 
-    def forward(buffer, block, way, k, send, recv):
-        place = buffer.at[block, part_rows(piece_of(way, k))]
-        remote(place, place, send.at[0], recv.at[way, k], cand=toward(way)).start()
+    def relay(source, target, block, distance, way, k, send, recv, **device):
+        place = part_rows(piece_of(way, k))
+        if distance < middle - 1 or (distance == middle - 1 and k < pieces // 2):
+            remote(
+                source.at[block, place],
+                target.at[block, place],
+                send.at[0],
+                recv.at[way, distance * pieces + k],
+                cand=toward(way),
+                **device,
+            ).start()
 
     def gather_step(buffer, k, send, recv):
         distance = k // pieces + 1
         for way in (0, 1):
             block = wrap(z - distance + 2 * distance * way)
             wait_bytes(buffer.at[block, part_rows(piece_of(way, k))], recv.at[way, k])
-            if k + pieces < messages:
-                forward(buffer, block, way, k + pieces, send, recv)
+            relay(buffer, buffer, block, distance, way, k % pieces, send, recv)
+
+    start_order = []
+    for q in range(pieces // 2):
+        start_order += [q, pieces - 1 - q]
+    ready = []
+    for n in range(pieces):
+        done = set(start_order[: n + 1])
+        fresh = []
+        for way in (0, 1):
+            for k in range(pieces):
+                before = all(piece_of(way, b) in done for b in range(k + 1))
+                if before and not any((way, k) in earlier for earlier in ready):
+                    fresh.append((way, k))
+        ready.append(fresh)
+
+    def relay_ready(buffer, n, send, recv):
+        for way, k in ready[n]:
+            relay(buffer, buffer, z, 0, way, k, send, recv)
 
     lane = lax.broadcasted_iota(jnp.int32, (T, LANES), 1)
     keep = (lax.broadcasted_iota(jnp.int32, (1, LANES), 1) < kept[0, 0]).astype(F32)
@@ -282,16 +307,15 @@
         def _():
             wait_bytes(x_buf.at[z], in_recv.at[0])
 
-        for q in range(pieces):
+        for n, q in enumerate(start_order):
 
             @pl.when(s > 0)
             def _(q=q):
                 wait_bytes(x_buf.at[z, part_rows(q)], nx_recv.at[q])
 
             @pl.when(jnp.logical_not(odd))
-            def _(q=q):
-                forward(x_buf, z, 0, q, ag_send, ag_recv)
-                forward(x_buf, z, 1, pieces - 1 - q, ag_send, ag_recv)
+            def _(n=n):
+                relay_ready(x_buf, n, ag_send, ag_recv)
 
         project(z)
         for j in range(middle):
@@ -361,36 +385,51 @@
         wait_bytes(s_recv.at[way, k], rs_recv.at[way, k])
         return s_recv[way, k].astype(F32)
 
-    def emit(slot, way, k):
-        value = part[slot, part_rows(piece_of(way, k)), :]
-        if k >= pieces:
-            value += got(way, k - pieces)
-        s_send[way, k] = value.astype(BF16)
+    def slot_of(offset, k):
+        return pieces // 2 + (middle - 1 - offset) * pieces + k
+
+    def contribution(offset, way, k):
+        if offset < middle - 1:
+            return got(way, slot_of(offset + 1, k))
+        return got(way, k) if k < pieces // 2 else 0.0
+
+    def emit(way, slot, value):
+        s_send[way, slot] = value.astype(BF16)
         remote(
-            s_send.at[way, k],
-            s_recv.at[way, k],
+            s_send.at[way, slot],
+            s_recv.at[way, slot],
             rs_send.at[0],
-            rs_recv.at[way, k],
+            rs_recv.at[way, slot],
             cand=toward(way),
         ).start()
+
+    arrival_order = list(range(pieces // 2, pieces)) + list(range(pieces // 2))
+
+    def mate_copies():
+        for d in range(1, N):
+            place = wrap(z + d)
+            remote(
+                x_buf.at[place], st_buf.at[place], mate_send.at[0], mate_recv.at[d], section=s - 1
+            ).start()
 
     def output():
         project_out(0, middle)
         for k in range(pieces // 2):
-            emit(0, 0, k)
-            emit(0, 1, k)
-        for j, m in enumerate(range(middle - 1, 0, -1)):
+            for way in (0, 1):
+                emit(way, k, part[0, part_rows(piece_of(way, k)), :])
+        for m in range(middle - 1, 0, -1):
             project_out(0, m)
             project_out(1, -m)
-            for k in range(pieces // 2 + j * pieces, pieces // 2 + (j + 1) * pieces):
-                emit(0, 0, k)
-                emit(1, 1, k)
+            for k in arrival_order:
+                for way in (0, 1):
+                    value = part[way, part_rows(piece_of(way, k)), :]
+                    emit(way, slot_of(m, k), value + contribution(m, way, k))
         project_out(0, 0)
         part[0] += x_buf[z].astype(F32)
-        for k in range(messages - pieces, messages):
+        for k in arrival_order:
             for way in (0, 1):
                 place = part_rows(piece_of(way, k))
-                total = part[0, place, :] + got(way, k)
+                total = part[0, place, :] + contribution(0, way, k)
                 part[0, place, :] = total
 
     def hand_over():
@@ -400,19 +439,11 @@
         def _():
             for k in range(pieces):
                 for way in (0, 1):
-                    place = part_rows(piece_of(way, k))
-                    remote(
-                        st_buf.at[z, place],
-                        x_buf.at[z, place],
-                        nx_send.at[0],
-                        ag_recv.at[way, k],
-                        section=s + 1,
-                        cand=toward(way),
-                    ).start()
+                    relay(st_buf, x_buf, z, 0, way, k, nx_send, ag_recv, section=s + 1)
 
         @pl.when(s < S - 1)
         def _():
-            for q in range(pieces):
+            for q in start_order:
                 remote(
                     st_buf.at[z, part_rows(q)],
                     x_buf.at[z, part_rows(q)],
@@ -423,19 +454,17 @@
 
         @pl.when(odd)
         def _():
-            for q in range(pieces):
-                forward(st_buf, z, 0, q, sg_send, sg_recv)
-                forward(st_buf, z, 1, pieces - 1 - q, sg_send, sg_recv)
-            for d in range(1, N):
-                place = x_buf.at[wrap(z + d)]
-                remote(
-                    place,
-                    st_buf.at[wrap(z + d)],
-                    mate_send.at[0],
-                    mate_recv.at[d],
-                    section=s - 1,
-                ).start()
-
+            @pl.when(s < S - 1)
+            def _():
+                wait_bytes(x_buf.at[0], nx_send.at[0])
+
+            for k in range(pieces):
+                for way in (0, 1):
+                    relay(st_buf, st_buf, z, 0, way, k, sg_send, sg_recv)
+
+        pl.when(odd)(mate_copies)
+
+    def send_state():
         for t in range(N):
             source = st_buf.at[z, pl.ds(t * piece, piece)]
             target = y_buf.at[rows(z)]
@@ -476,6 +505,8 @@
             def _(j=j):
                 for k in range(j * pieces, min((j + 1) * pieces, messages)):
                     gather_step(st_buf, k, sg_send, sg_recv)
+                if j == middle - 2:
+                    send_state()
 
             @pl.when(jnp.logical_not(odd))
             def _(j=j, last=last):
@@ -486,6 +517,7 @@
             candidate(wrap(z + j + 1))
             if not last:
                 candidate(wrap(z - j - 1))
+
 
     def gradients():
         wait_bytes(bw_recv.at[pl.ds(0, N - 1)], b_recv.at[0])
@@ -504,6 +536,7 @@
         g_up[...] = dot_tn(hidden_all, sc_buf[...].reshape(N * T, F))
         up_copy = pltpu.make_async_copy(g_up.at[pl.ds(0, R)], up_out.at[0, 0], load_sem.at[0])
         up_copy.start()
+        pl.when(jnp.logical_not(odd))(send_state)
         wait_bytes(y_buf, y_recv.at[0])
         y_copy = pltpu.make_async_copy(y_buf, states_out.at[0], load_sem.at[1])
         y_copy.start()
@@ -537,10 +570,6 @@
             wait_bytes(x_buf.at[pl.ds(0, N - 3)], ag_send.at[0])
             wait_bytes(st_buf.at[others], sg_send.at[0])
             wait_bytes(st_buf.at[others], mate_send.at[0])
-
-            @pl.when(s < S - 1)
-            def _():
-                wait_bytes(x_buf.at[0], nx_send.at[0])
 
         wait_bytes(p_buf.at[others], p_send.at[0])
         wait_bytes(a_buf.at[others], a_send.at[0])

time: 252 us -> 230 us (0.913)
  Pallas kernels: 246 us -> 224 us
    pallas_call x1, Pallas kernels: 246 us -> 224 us  [shards(): pl.pallas_call(functools.partial(body, N, S, sharing), out_shape=(jax.Sha...]
where the time goes in v3:
time: 230 us
  Pallas kernels  224 us (97%)
  local copies, waits for them, and re-layouts  5.01 us (2%)
    pallas_call x1, Pallas kernels, shards(): pl.pallas_call(functools.partial(body, N, S, sharing), out_shape=(jax.Sha...  224 us
    unnamed x3, local copies, waits for them, and re-layouts  5.01 us

profile of v3, /device:TPU:29, one launch (start us, length us, event | category | flops | bytes accessed | tf_op | source)
XLA Modules:
  0.0 230.0 jit_solution(2275609524368318098)
XLA Ops:
  1.3 223.7 %shard_map.130 = (bf16[1,128,1024]{2,1,0:T(8,128)(2,1)}, f32[1,1,64,1024]{3,2,1,0:T(8,128)}, f32[1,1,64,1024]{3,2,1,0:T(8,128)}) custom-call(bf16[128,1024]{1,0:T(8,128)(2,1)} %inputs.1, f32[1,8192]{1,0:T(1,128)} %parent_gain.1, bf16[1,1024,512]{2,1,0:T(8,128)(2,1)} %query_weight.1, bf16[1,2,1024,512]{3,2,1,0:T(8,128)(2,1)} %key_value_weight.1, ...), custom_call_target="tpu_custom_call" | custom-call | tf_op jit(solution)/shard_map/pallas_call | solution.py:618
  225.0 1.7 copy.18
  226.7 1.7 copy.19
  228.3 1.7 copy.20

commit v4 on v3

--- a/solution.py
+++ b/solution.py
@@ -76,6 +76,9 @@
     bw_send,
     bw_recv,
     bw_all,
+    last_send,
+    last_recv,
+    y_mid,
     y_buf,
     g_down,
     g_up,
@@ -102,6 +105,10 @@
     b_recv,
     c_send,
     c_recv,
+    d_send,
+    d_recv,
+    m_send,
+    m_recv,
 ):
     s = lax.axis_index("section")
     z = lax.axis_index("cand")
@@ -163,9 +170,8 @@
 
     diagonal = i == z
     odd = lax.rem(s, 2) == 1
-    greet(cand=wrap(z + 1))
-    greet(cand=wrap(z - 1))
     for k in range(1, N):
+        greet(cand=wrap(z + k))
         greet(dp=wrap(i + k))
     for w in range(N):
 
@@ -187,8 +193,8 @@
     greet(section=mate, cand=wrap(z - 1))
 
     expected = (
-        4
-        + (N - 1)
+        2
+        + 2 * (N - 1)
         + 2 * N
         - 2 * diagonal.astype(jnp.int32)
         + (s > 0).astype(jnp.int32)
@@ -272,9 +278,9 @@
                     fresh.append((way, k))
         ready.append(fresh)
 
-    def relay_ready(buffer, n, send, recv):
+    def relay_ready(source, target, n, send, recv, **device):
         for way, k in ready[n]:
-            relay(buffer, buffer, z, 0, way, k, send, recv)
+            relay(source, target, z, 0, way, k, send, recv, **device)
 
     lane = lax.broadcasted_iota(jnp.int32, (T, LANES), 1)
     keep = (lax.broadcasted_iota(jnp.int32, (1, LANES), 1) < kept[0, 0]).astype(F32)
@@ -302,6 +308,12 @@
             ).start()
         r_buf[i, rows(block), :] = p_buf[block, rows(i), :]
 
+    def mate_copy(d):
+        place = wrap(z + d)
+        remote(
+            x_buf.at[place], st_buf.at[place], mate_send.at[0], mate_recv.at[d], section=s - 1
+        ).start()
+
     def gather_and_project():
         @pl.when(s == 0)
         def _():
@@ -315,7 +327,7 @@
 
             @pl.when(jnp.logical_not(odd))
             def _(n=n):
-                relay_ready(x_buf, n, ag_send, ag_recv)
+                relay_ready(x_buf, x_buf, n, ag_send, ag_recv)
 
         project(z)
         for j in range(middle):
@@ -324,6 +336,12 @@
             project(wrap(z + j + 1))
             if j < middle - 1:
                 project(wrap(z - j - 1))
+
+                @pl.when(odd)
+                def _(j=j):
+                    mate_copy(j + 1)
+                    mate_copy(N - j - 1)
+
 
     def summed(b):
         total = r_buf[0, :, pl.ds(b * LANES, LANES)].astype(F32)
@@ -405,12 +423,27 @@
 
     arrival_order = list(range(pieces // 2, pieces)) + list(range(pieces // 2))
 
-    def mate_copies():
-        for d in range(1, N):
-            place = wrap(z + d)
-            remote(
-                x_buf.at[place], st_buf.at[place], mate_send.at[0], mate_recv.at[d], section=s - 1
-            ).start()
+    def next_piece(q):
+        remote(
+            st_buf.at[z, part_rows(q)],
+            x_buf.at[z, part_rows(q)],
+            nx_send.at[0],
+            nx_recv.at[q],
+            section=s + 1,
+        ).start()
+
+    def hand_on(n):
+        @pl.when(jnp.logical_not(odd))
+        def _():
+            relay_ready(st_buf, x_buf, n, nx_send, ag_recv, section=s + 1)
+
+        @pl.when(odd & (s < S - 1))
+        def _():
+            next_piece(start_order[n])
+
+        @pl.when(s == S - 1)
+        def _():
+            relay_ready(st_buf, st_buf, n, sg_send, sg_recv)
 
     def output():
         project_out(0, middle)
@@ -425,66 +458,67 @@
                     value = part[way, part_rows(piece_of(way, k)), :]
                     emit(way, slot_of(m, k), value + contribution(m, way, k))
         project_out(0, 0)
-        part[0] += x_buf[z].astype(F32)
-        for k in arrival_order:
+        for n, q in enumerate(start_order):
+            place = part_rows(q)
+            total = x_buf[z, place, :].astype(F32) + part[0, place, :]
             for way in (0, 1):
-                place = part_rows(piece_of(way, k))
-                total = part[0, place, :] + contribution(0, way, k)
-                part[0, place, :] = total
+                total += contribution(0, way, piece_of(way, q))
+            st_buf[z, place, :] = total.astype(BF16)
+            hand_on(n)
 
     def hand_over():
-        st_buf[z] = part[0].astype(BF16)
-
-        @pl.when(jnp.logical_not(odd))
-        def _():
-            for k in range(pieces):
-                for way in (0, 1):
-                    relay(st_buf, x_buf, z, 0, way, k, nx_send, ag_recv, section=s + 1)
-
-        @pl.when(s < S - 1)
-        def _():
-            for q in start_order:
-                remote(
-                    st_buf.at[z, part_rows(q)],
-                    x_buf.at[z, part_rows(q)],
-                    nx_send.at[0],
-                    nx_recv.at[q],
-                    section=s + 1,
-                ).start()
-
         @pl.when(odd)
         def _():
             @pl.when(s < S - 1)
             def _():
                 wait_bytes(x_buf.at[0], nx_send.at[0])
-
-            for k in range(pieces):
-                for way in (0, 1):
-                    relay(st_buf, st_buf, z, 0, way, k, sg_send, sg_recv)
-
-        pl.when(odd)(mate_copies)
+                for n in range(pieces):
+                    relay_ready(st_buf, st_buf, n, sg_send, sg_recv)
+
+            mate_copy(middle)
+
+        send_state()
+
+        @pl.when(jnp.logical_not(odd))
+        def _():
+            for q in range(pieces):
+                next_piece(q)
 
     def send_state():
-        for t in range(N):
-            source = st_buf.at[z, pl.ds(t * piece, piece)]
-            target = y_buf.at[rows(z)]
-            own = diagonal & (i == t)
-
-            @pl.when(own)
-            def _(source=source, target=target):
-                pltpu.make_async_copy(source, target, y_recv.at[0]).start()
-
-            @pl.when(jnp.logical_not(own))
-            def _(source=source, target=target, t=t):
-                remote(source, target, y_send.at[0], y_recv.at[0], dp=t, cand=i).start()
-
-    def candidate(block):
+        for k in range(1, N):
+            t = wrap(i + k)
+            remote(
+                st_buf.at[z, rows(t)], y_mid.at[i], m_send.at[0], m_recv.at[0], dp=t
+            ).start()
+        y_mid[i] = st_buf[z, rows(i), :]
+
+    def pass_state():
+        wait_bytes(y_mid.at[pl.ds(0, N - 1)], m_recv.at[0])
+        for k in range(1, N):
+            w = wrap(z + k)
+            remote(
+                y_mid.at[w], y_buf.at[rows(z)], y_send.at[0], y_recv.at[0], cand=w
+            ).start()
+        y_buf[rows(z), :] = y_mid[z]
+
+    farthest = wrap(z + middle)
+
+    def candidate(block, last=False):
         hidden = a_buf[block, :, pl.ds(QW, LANES)]
         branch = jnp.dot(hidden, w_up[...], preferred_element_type=F32)
         difference = branch - (st_buf[block].astype(F32) - x_buf[block].astype(F32))
         scaled = (difference * (1.0 / token_total)).astype(BF16)
         sc_buf[block] = scaled
-        bw_send[block] = dot_nt(scaled, w_up[...]).astype(BF16)
+        backward = dot_nt(scaled, w_up[...]).astype(BF16)
+        if last:
+            last_send[...] = backward
+            for k in range(1, N):
+                remote(
+                    last_send, last_recv.at[i], d_send.at[0], d_recv.at[0], dp=wrap(i + k)
+                ).start()
+            last_recv[i] = backward
+            return
+        bw_send[block] = backward
 
         @pl.when(block == i)
         def _():
@@ -497,6 +531,10 @@
             ).start()
 
     def candidates():
+        @pl.when(jnp.logical_not(odd))
+        def _():
+            wait_bytes(st_buf.at[wrap(z + middle)], mate_recv.at[middle])
+
         candidate(z)
         for j in range(middle):
             last = j == middle - 1
@@ -505,43 +543,53 @@
             def _(j=j):
                 for k in range(j * pieces, min((j + 1) * pieces, messages)):
                     gather_step(st_buf, k, sg_send, sg_recv)
-                if j == middle - 2:
-                    send_state()
 
             @pl.when(jnp.logical_not(odd))
             def _(j=j, last=last):
-                wait_bytes(st_buf.at[wrap(z + j + 1)], mate_recv.at[j + 1])
                 if not last:
+                    wait_bytes(st_buf.at[wrap(z + j + 1)], mate_recv.at[j + 1])
                     wait_bytes(st_buf.at[wrap(z - j - 1)], mate_recv.at[N - j - 1])
 
-            candidate(wrap(z + j + 1))
+            candidate(wrap(z + j + 1), last)
             if not last:
                 candidate(wrap(z - j - 1))
 
 
     def gradients():
-        wait_bytes(bw_recv.at[pl.ds(0, N - 1)], b_recv.at[0])
-        backward = bw_recv[0].astype(F32)
-        for source in range(1, N):
-            backward += bw_recv[source].astype(F32)
-        own_extra = a_buf[i, :, pl.ds(QW, LANES)].astype(F32)
-        own_inverse = own_extra[:, R : R + 1] + own_extra[:, R + 1 : R + 2]
-        bw_all[i] = (backward * keep * own_inverse).astype(BF16)
-        for k in range(1, N):
-            remote(
-                bw_all.at[i], bw_all.at[i], c_send.at[0], c_recv.at[0], dp=wrap(i + k)
-            ).start()
+        def finish(block, received):
+            backward = received[0].astype(F32)
+            for source in range(1, N):
+                backward += received[source].astype(F32)
+            extra = a_buf[block, :, pl.ds(QW, LANES)].astype(F32)
+            inverse = extra[:, R : R + 1] + extra[:, R + 1 : R + 2]
+            bw_all[block] = (backward * keep * inverse).astype(BF16)
+
+        @pl.when(i != farthest)
+        def _():
+            wait_bytes(bw_recv.at[pl.ds(0, N - 1)], b_recv.at[0])
+            finish(i, bw_recv)
+            for k in range(1, N):
+                remote(
+                    bw_all.at[i], bw_all.at[i], c_send.at[0], c_recv.at[0], dp=wrap(i + k)
+                ).start()
 
         hidden_all = a_buf[:, :, pl.ds(QW, LANES)].reshape(N * T, LANES)
         g_up[...] = dot_tn(hidden_all, sc_buf[...].reshape(N * T, F))
         up_copy = pltpu.make_async_copy(g_up.at[pl.ds(0, R)], up_out.at[0, 0], load_sem.at[0])
         up_copy.start()
-        pl.when(jnp.logical_not(odd))(send_state)
-        wait_bytes(y_buf, y_recv.at[0])
-        y_copy = pltpu.make_async_copy(y_buf, states_out.at[0], load_sem.at[1])
-        y_copy.start()
-
-        wait_bytes(bw_all.at[pl.ds(0, N - 1)], c_recv.at[0])
+        pass_state()
+
+        wait_bytes(last_recv.at[pl.ds(0, N - 1)], d_recv.at[0])
+        finish(farthest, last_recv)
+
+        @pl.when(i != farthest)
+        def _():
+            wait_bytes(bw_all.at[pl.ds(0, N - 2)], c_recv.at[0])
+
+        @pl.when(i == farthest)
+        def _():
+            wait_bytes(bw_all.at[pl.ds(0, N - 1)], c_recv.at[0])
+
         g_down[...] = (
             dot_tn(bw_all[...].reshape(N * T, LANES), x_buf[...].reshape(N * T, F)) * cg[...]
         )
@@ -549,6 +597,9 @@
             g_down.at[pl.ds(0, R)], down_out.at[0, 0], load_sem.at[2]
         )
         down_copy.start()
+        wait_bytes(y_buf.at[pl.ds(0, T - piece)], y_recv.at[0])
+        y_copy = pltpu.make_async_copy(y_buf, states_out.at[0], load_sem.at[1])
+        y_copy.start()
         up_copy.wait()
         y_copy.wait()
         down_copy.wait()
@@ -574,9 +625,18 @@
         wait_bytes(p_buf.at[others], p_send.at[0])
         wait_bytes(a_buf.at[others], a_send.at[0])
         wait_bytes(s_send, rs_send.at[0])
-        wait_pieces_sent(y_send.at[0])
-        wait_bytes(bw_send.at[others], b_send.at[0])
-        wait_bytes(bw_all.at[others], c_send.at[0])
+        wait_bytes(y_mid.at[others], m_send.at[0])
+        wait_bytes(y_mid.at[others], y_send.at[0])
+        wait_bytes(last_recv.at[others], d_send.at[0])
+
+        @pl.when(i != farthest)
+        def _():
+            wait_bytes(bw_send.at[pl.ds(0, N - 2)], b_send.at[0])
+            wait_bytes(bw_all.at[others], c_send.at[0])
+
+        @pl.when(i == farthest)
+        def _():
+            wait_bytes(bw_send.at[others], b_send.at[0])
 
     @pl.when(s == 0)
     def _():
@@ -646,6 +706,9 @@
             pltpu.VMEM((N, T, LANES), BF16),
             pltpu.VMEM((N, T, LANES), BF16),
             pltpu.VMEM((N, T, LANES), BF16),
+            pltpu.VMEM((T, LANES), BF16),
+            pltpu.VMEM((N, T, LANES), BF16),
+            pltpu.VMEM((N, T // N, F), BF16),
             pltpu.VMEM((T, F), BF16),
             pltpu.VMEM((LANES, F), F32),
             pltpu.VMEM((LANES, F), F32),
@@ -666,6 +729,10 @@
             dma((2, messages)),
             dma((1,)),
             dma((N,)),
+            dma((1,)),
+            dma((1,)),
+            dma((1,)),
+            dma((1,)),
             dma((1,)),
             dma((1,)),
             dma((1,)),

time: 230 us -> 208 us (0.904)
  Pallas kernels: 224 us -> 201 us
    pallas_call x1, Pallas kernels: 224 us -> 201 us  [shards(): pl.pallas_call(functools.partial(body, N, S, sharing), out_shape=(jax.Sha...]
where the time goes in v4:
time: 208 us; the launch traced here: 207 us
  Pallas kernels  201 us (97%)
  local copies, waits for them, and re-layouts  5.01 us (2%)
    pallas_call x1, Pallas kernels, shards(): pl.pallas_call(functools.partial(body, N, S, sharing), out_shape=(jax.Sha...  201 us
    unnamed x3, local copies, waits for them, and re-layouts  5.01 us

profile of v4, /device:TPU:29, one launch (start us, length us, event | category | flops | bytes accessed | tf_op | source)
XLA Modules:
  0.0 207.1 jit_solution(212063985534086232)
XLA Ops:
  1.3 200.8 %shard_map.130 = (bf16[1,128,1024]{2,1,0:T(8,128)(2,1)}, f32[1,1,64,1024]{3,2,1,0:T(8,128)}, f32[1,1,64,1024]{3,2,1,0:T(8,128)}) custom-call(bf16[128,1024]{1,0:T(8,128)(2,1)} %inputs.1, f32[1,8192]{1,0:T(1,128)} %parent_gain.1, bf16[1,1024,512]{2,1,0:T(8,128)(2,1)} %query_weight.1, bf16[1,2,1024,512]{3,2,1,0:T(8,128)(2,1)} %key_value_weight.1, ...), custom_call_target="tpu_custom_call" | custom-call | tf_op jit(solution)/shard_map/pallas_call | solution.py:678
  202.1 1.7 copy.18
  203.8 1.7 copy.19
  205.5 1.7 copy.20

commit v5 on v4

--- a/solution.py
+++ b/solution.py
@@ -10,7 +10,7 @@
 
 HD = 128
 LANES = 128
-PIECES = 4
+PIECES = 8
 EPSILON = 1e-05
 ROPE_BASE = 500000.0
 MESH = pl.DeviceIdType.MESH

time: 208 us -> 205 us (0.986)
  Pallas kernels: 201 us -> 198 us
    pallas_call x1, Pallas kernels: 201 us -> 198 us  [shards(): pl.pallas_call(functools.partial(body, N, S, sharing), out_shape=(jax.Sha...]
where the time goes in v5:
time: 205 us; the launch traced here: 204 us
  Pallas kernels  198 us (97%)
  local copies, waits for them, and re-layouts  5.01 us (2%)
    pallas_call x1, Pallas kernels, shards(): pl.pallas_call(functools.partial(body, N, S, sharing), out_shape=(jax.Sha...  198 us
    unnamed x3, local copies, waits for them, and re-layouts  5.01 us

profile of v5, /device:TPU:29, one launch (start us, length us, event | category | flops | bytes accessed | tf_op | source)
XLA Modules:
  0.0 204.0 jit_solution(7776869586431913465)
XLA Ops:
  1.3 197.7 %shard_map.130 = (bf16[1,128,1024]{2,1,0:T(8,128)(2,1)}, f32[1,1,64,1024]{3,2,1,0:T(8,128)}, f32[1,1,64,1024]{3,2,1,0:T(8,128)}) custom-call(bf16[128,1024]{1,0:T(8,128)(2,1)} %inputs.1, f32[1,8192]{1,0:T(1,128)} %parent_gain.1, bf16[1,1024,512]{2,1,0:T(8,128)(2,1)} %query_weight.1, bf16[1,2,1024,512]{3,2,1,0:T(8,128)(2,1)} %key_value_weight.1, ...), custom_call_target="tpu_custom_call" | custom-call | tf_op jit(solution)/shard_map/pallas_call | solution.py:678
  199.0 1.7 copy.18
  200.6 1.7 copy.19
  202.3 1.7 copy.20

commit v6 on v5

--- a/solution.py
+++ b/solution.py
@@ -337,11 +337,6 @@
             if j < middle - 1:
                 project(wrap(z - j - 1))
 
-                @pl.when(odd)
-                def _(j=j):
-                    mate_copy(j + 1)
-                    mate_copy(N - j - 1)
-
 
     def summed(b):
         total = r_buf[0, :, pl.ds(b * LANES, LANES)].astype(F32)
@@ -391,6 +386,12 @@
                     dp=wrap(i + k),
                 ).start()
             a_buf[block, rows(i), :] = a_own[rows(block), :]
+
+        @pl.when(odd)
+        def _():
+            for d in range(1, N):
+                if d != middle:
+                    mate_copy(d)
 
     def project_out(slot, offset):
         block = wrap(z + offset)

time: 205 us -> 205 us (level)
  no operation moved by 1% of the time
where the time goes in v6:
time: 205 us; the launch traced here: 204 us
  Pallas kernels  198 us (97%)
  local copies, waits for them, and re-layouts  5.01 us (2%)
    pallas_call x1, Pallas kernels, shards(): pl.pallas_call(functools.partial(body, N, S, sharing), out_shape=(jax.Sha...  198 us
    unnamed x3, local copies, waits for them, and re-layouts  5.01 us

profile of v6, /device:TPU:29, one launch (start us, length us, event | category | flops | bytes accessed | tf_op | source)
XLA Modules:
  0.0 204.0 jit_solution(6414494133330131964)
XLA Ops:
  1.3 197.7 %shard_map.130 = (bf16[1,128,1024]{2,1,0:T(8,128)(2,1)}, f32[1,1,64,1024]{3,2,1,0:T(8,128)}, f32[1,1,64,1024]{3,2,1,0:T(8,128)}) custom-call(bf16[128,1024]{1,0:T(8,128)(2,1)} %inputs.1, f32[1,8192]{1,0:T(1,128)} %parent_gain.1, bf16[1,1024,512]{2,1,0:T(8,128)(2,1)} %query_weight.1, bf16[1,2,1024,512]{3,2,1,0:T(8,128)(2,1)} %key_value_weight.1, ...), custom_call_target="tpu_custom_call" | custom-call | tf_op jit(solution)/shard_map/pallas_call | solution.py:679
  199.0 1.7 copy.18
  200.6 1.7 copy.19
  202.3 1.7 copy.20
